TPU v7x, 256 devices: a whole 4x4x8 slice. The times are simulated.
256 devices in a mesh: dp: 4 (over x), seq: 16 (over z_hi, y, core), head: 4 (over z_lo).
Axes of the slice: x: 4, y: 4, z: 8 (z_hi: 2, z_lo: 4; z = z_hi * 4 + z_lo), core: 2. Of those that a mesh axis runs over, the one named last changes fastest.
Arguments:
- map_thirteen: bfloat16 [32, 16, 13, 1920], P('dp', 'seq'), may hold values from -6 to 6
- kv_cache: bfloat16 [32, 256, 2, 1024], P('dp', 'seq', None, 'head'), may hold values from -6 to 6
- class_labels: int32 [32], P('dp'), may hold values from 0 to 999
- class_table: bfloat16 [1000, 3, 1920], P('head'), may hold values from -4 to 4
- sampled_ids: int32 [32, 13, 13], P('dp'), may hold values from 0 to 4095
- codebook: float32 [4096, 32], replicated, may hold values from -6 to 6
- feature_sum: float32 [32, 16, 512], P('dp', 'seq'), may hold values from -6 to 6
- embed_weight: float32 [32, 1920], replicated, may hold values from -1 to 1
- embed_bias: float32 [1920], replicated, may hold values from -3 to 3
- position_table: bfloat16 [16, 16, 1920], P('seq'), may hold values from -3 to 3
- qkv_weight: bfloat16 [1920, 3, 1024], P(None, None, 'head'), may hold values from -0.125 to 0.125
- out_weight: bfloat16 [1024, 1920], P('head'), may hold values from -0.1875 to 0.1875
- head_scale: float32 [16], P('head'), may hold values from 2 to 40
Outputs:
- branch_thirteen: bfloat16 [32, 16, 13, 1920], P('dp', 'seq')
- branch_sixteen: bfloat16 [32, 16, 16, 1920], P('dp', 'seq')
All inputs are finite; a program needn't handle non-finite values.
Results may differ from a plain program's by a relative error of at most 0.011.
Values may be sent and summed in bfloat16 or wider, within the bound.
A program may use at most 64 MiB of HBM per device.

v0:
```python
import jax
import jax.numpy as jnp
import numpy as np
from jax import lax
from jax.sharding import PartitionSpec as P

S13 = 13
S16 = 16
COARSE = 255


def upsample_table():
    source = (np.arange(S16) + 0.5) * S13 / S16 - 0.5
    source = np.maximum(source, 0.0)
    lower = np.floor(source).astype(np.int32)
    upper = np.minimum(lower + 1, S13 - 1)
    weight = source - lower
    interp = np.zeros((S16, S13))
    interp[np.arange(S16), lower] += 1.0 - weight
    interp[np.arange(S16), upper] += weight
    return interp


def normalize(vectors):
    return vectors * lax.rsqrt(jnp.sum(vectors * vectors, axis=-1, keepdims=True) + 1e-06)


def accumulate(totals, queries, keys, values, usable):
    numerator, denominator = totals
    scores = jnp.einsum("bqhe,bkhe->bqhk", queries, keys, preferred_element_type=jnp.float32)
    weights = jnp.exp(scores) * usable
    denominator = denominator + jnp.sum(weights, axis=-1)
    numerator = numerator + jnp.einsum(
        "bqhk,bkhe->bqhe", weights.astype(jnp.bfloat16), values, preferred_element_type=jnp.float32
    )
    return (numerator, denominator)


def body(
    map_thirteen,
    kv_cache,
    class_labels,
    class_table,
    sampled_ids,
    codebook,
    feature_sum,
    embed_weight,
    embed_bias,
    position_table,
    qkv_weight,
    out_weight,
    head_scale,
):
    images = map_thirteen.shape[0]
    map_rows = map_thirteen.shape[1]
    model_width = map_thirteen.shape[3]
    width = out_weight.shape[0]
    heads_here = head_scale.shape[0]
    head_size = width // heads_here
    code_width = codebook.shape[1]
    row_start = lax.axis_index("seq") * map_rows
    owned = class_table.shape[0]
    class_start = lax.axis_index("head") * owned
    onehot = (
        class_labels[:, None] == class_start + jnp.arange(owned, dtype=jnp.int32)[None, :]
    ).astype(jnp.bfloat16)
    partial_rows = jnp.einsum(
        "bc,ctd->btd", onehot, class_table, preferred_element_type=jnp.float32
    )
    modulation = lax.psum(partial_rows.astype(jnp.bfloat16), "head").astype(jnp.float32)
    interp = jnp.asarray(upsample_table(), jnp.float32)
    local_rows = lax.dynamic_slice_in_dim(interp, row_start, map_rows, 0)
    looked_up = codebook[sampled_ids]
    upsampled = jnp.einsum("ri,bijc->brjc", local_rows, looked_up, precision=lax.Precision.HIGHEST)
    upsampled = jnp.einsum("sj,brjc->brsc", interp, upsampled, precision=lax.Precision.HIGHEST)
    features = feature_sum.reshape(images, map_rows, S16, code_width) + upsampled
    embedded = jnp.einsum("brsc,cd->brsd", features, embed_weight, precision=lax.Precision.HIGHEST)
    map_sixteen = (embedded + embed_bias + position_table.astype(jnp.float32)).astype(jnp.bfloat16)
    small_count = map_rows * S13
    large_count = map_rows * S16
    total_rows = small_count + large_count
    inputs = jnp.concatenate(
        [
            map_thirteen.reshape(images, small_count, model_width),
            map_sixteen.reshape(images, large_count, model_width),
        ],
        axis=1,
    ).astype(jnp.float32)
    centred = inputs - jnp.mean(inputs, axis=-1, keepdims=True)
    variance = jnp.mean(centred * centred, axis=-1, keepdims=True)
    modulated = (
        centred * lax.rsqrt(variance + 1e-06) * (1.0 + modulation[:, 1][:, None, :])
        + modulation[:, 0][:, None, :]
    ).astype(jnp.bfloat16)
    projected = jnp.einsum(
        "bnd,dk->bnk",
        modulated,
        qkv_weight.reshape(model_width, 3 * width),
        preferred_element_type=jnp.float32,
    )
    projected = projected.reshape(images, total_rows, 3, heads_here, head_size)
    queries = (normalize(projected[:, :, 0]) * head_scale[None, None, :, None]).astype(jnp.bfloat16)
    keys = normalize(projected[:, :, 1]).astype(jnp.bfloat16)
    values = projected[:, :, 2].astype(jnp.bfloat16)
    fine_small = jnp.stack([keys[:, :small_count], values[:, :small_count]], axis=2).reshape(
        images, map_rows, S13, 2, width
    )
    fine_large = jnp.stack([keys[:, small_count:], values[:, small_count:]], axis=2).reshape(
        images, map_rows, S16, 2, width
    )
    slots_here = kv_cache.shape[1]
    cache_keys = normalize(
        kv_cache[:, :, 0].astype(jnp.float32).reshape(images, slots_here, heads_here, head_size)
    ).astype(jnp.bfloat16)
    coarse_local = jnp.stack(
        [cache_keys.reshape(images, slots_here, width), kv_cache[:, :, 1]], axis=2
    )
    later_rows = (
        (jnp.arange(total_rows, dtype=jnp.int32) >= small_count)
        .astype(jnp.float32)
        .reshape(1, total_rows, 1, 1)
    )
    empty = (
        jnp.zeros((images, total_rows, heads_here, head_size), jnp.float32),
        jnp.zeros((images, total_rows, heads_here), jnp.float32),
    )
    pieces = lax.all_gather(coarse_local, "seq", axis=1, tiled=True)
    piece_rows = pieces.shape[1]
    usable = (
        (jnp.arange(piece_rows, dtype=jnp.int32) < COARSE)
        .astype(jnp.float32)
        .reshape(1, 1, 1, piece_rows)
    )
    piece_keys = pieces[:, :, 0].reshape(images, piece_rows, heads_here, head_size)
    piece_values = pieces[:, :, 1].reshape(images, piece_rows, heads_here, head_size)
    coarse_num, coarse_den = accumulate(empty, queries, piece_keys, piece_values, usable)
    totals = empty
    small_piece = lax.all_gather(fine_small, "seq", axis=1, tiled=True)
    large_piece = lax.all_gather(fine_large, "seq", axis=1, tiled=True)
    piece_rows = small_piece.shape[1]
    row_ok = (jnp.arange(piece_rows, dtype=jnp.int32) < S13).astype(jnp.float32)
    usable = jnp.repeat(row_ok, S13).reshape(1, 1, 1, piece_rows * S13)
    small_keys = small_piece[:, :, :, 0].reshape(images, piece_rows * S13, heads_here, head_size)
    small_values = small_piece[:, :, :, 1].reshape(images, piece_rows * S13, heads_here, head_size)
    totals = accumulate(totals, queries, small_keys, small_values, usable)
    large_keys = large_piece[:, :, :, 0].reshape(images, piece_rows * S16, heads_here, head_size)
    large_values = large_piece[:, :, :, 1].reshape(images, piece_rows * S16, heads_here, head_size)
    fine_num, fine_den = accumulate(totals, queries, large_keys, large_values, later_rows)
    numerator = coarse_num + fine_num
    denominator = coarse_den + fine_den
    attended = (
        (numerator / denominator[..., None]).astype(jnp.bfloat16).reshape(images, total_rows, width)
    )
    partial_branch = jnp.einsum(
        "bnk,kd->bnd", attended, out_weight, preferred_element_type=jnp.float32
    )
    partial_small = partial_branch[:, :small_count]
    partial_large = partial_branch[:, small_count:]
    gate_rows = modulation[:, 2]
    summed_small, summed_large = lax.psum((partial_small, partial_large), "head")
    gated_small = (gate_rows[:, None, :] * summed_small).astype(jnp.bfloat16)
    gated_large = (gate_rows[:, None, :] * summed_large).astype(jnp.bfloat16)
    kept_rows = (row_start + jnp.arange(map_rows, dtype=jnp.int32) < S13)[None, :, None, None]
    branch_thirteen = gated_small.reshape(images, map_rows, S13, model_width)
    branch_thirteen = jnp.where(kept_rows, branch_thirteen, jnp.zeros_like(branch_thirteen))
    branch_sixteen = gated_large.reshape(images, map_rows, S16, model_width)
    return (branch_thirteen, branch_sixteen)


def solution(mesh):
    placed = (
        P("dp", "seq", None, None),
        P("dp", "seq", None, "head"),
        P("dp"),
        P("head", None, None),
        P("dp", None, None),
        P(),
        P("dp", "seq", None),
        P(),
        P(),
        P("seq", None, None),
        P(None, None, "head"),
        P("head", None),
        P("head"),
    )
    return jax.shard_map(
        body,
        mesh=mesh,
        in_specs=placed,
        out_specs=(P("dp", "seq", None, None), P("dp", "seq", None, None)),
        check_vma=False,
    )
```

profile of v0, /device:TPU:1, one launch (start us, length us, event | category | flops | bytes accessed | tf_op | source)
XLA Modules:
  0.0 380.2 jit_solution(10410400588036335149)
XLA Ops:
  7.3 1.7 copy-done
  9.0 1.8 convolution_convert_fusion
  11.1 1.9 copy.50
  13.0 0.8 compare_select_fusion
  14.0 5.2 %gather_fusion = f32[1352,32]{1,0:T(8,128)} fusion(f32[4096,32]{1,0:T(8,128)} %copy.50, s32[2048]{0:T(1024)S(1)} %pad_clamp_fusion), kind=kCustom, calls=%fused_computation | custom fusion | bytes 351520 | tf_op jit(solution)/shard_map/gather | solution.py:73
  19.3 2.1 reshape.138
  22.1 1.0 copy.111
  23.1 2.1 fusion.53
  25.4 1.9 fusion.1
  28.7 4.7 %copy.51 = bf16[1920,3,256]{0,2,1:T(8,128)(2,1)} copy(bf16[1920,3,256]{2,0,1:T(8,128)(2,1)} %param.24) | data formatting | bytes 5898240 | tf_op args[10]
  33.4 27.8 %all-reduce.4.cloned.1.call-done = bf16[8,3,1920]{2,0,1:T(8,128)(2,1)} async-done(((bf16[8,3,1920]{2,0,1:T(8,128)(2,1)}), bf16[8,3,1920]{2,0,1:T(8,128)(2,1)}) %all-reduce.4.cloned.1.call-update) | async-done | bytes 92176 | tf_op jit(solution)/shard_map/psum | solution.py:70
  61.2 0.9 convert_element_type.78
  62.2 3.8 %fusion.45 = f32[8,29,3,4,64]{4,1,3,2,0:T(8,128)S(1)} fusion(bf16[3,4,64,1920,1]{3,2,1,0,4:T(8,128)(2,1)} %bitcast.132, f32[8,1920]{1,0:T(8,128)S(1)} %get-tuple-element.21, f32[8,1920]{1,0:T(8,128)S(1)} %get-tuple-element.22, f32[8,29]{1,0:T(8,128)S(1)} %add_rsqrt_fusion.3, f32[8,29]{1,0:T(8,128)S(1)} %broadcast_multiply_fusion, ...), kind=kOutput, calls=%fused_computation.39 | convolution fusion | flops 688204800 | bytes 4677440 | tf_op jit(solution)/shard_map/bnd,dk->bnk/dot_general | solution.py:95
  66.1 1.1 copy-done.3
  68.1 2.2 multiply_convert_fusion.3
  70.4 0.7 copy-done.7
  73.6 1.1 mul.132
  75.1 0.9 mul.134
  75.9 0.9 fusion.63
  76.9 1.5 pad_maximum_fusion.2
  78.4 1.0 slice.96
  79.4 1.0 slice.95
  82.0 51.4 %all-gather.6.cloned.1.call-done = bf16[8,16,13,2,256]{4,0,3,2,1:T(8,128)(2,1)} async-done(((bf16[8,1,13,2,256]{4,0,3,2,1:T(8,128)(2,1)}), bf16[8,16,13,2,256]{4,0,3,2,1:T(8,128)(2,1)}) %all-gather.6.cloned.1.call-update) | async-done | bytes 1703952 | tf_op jit(solution)/shard_map/all_gather | solution.py:138
  133.4 2.8 fusion.77
  136.1 3.8 reshape_squeeze.20
  139.9 3.7 reshape_squeeze.21
  143.7 3.5 fusion.80
  147.2 48.1 %all-gather.4.cloned.1.call-done = bf16[8,256,2,256]{3,1,0,2:T(8,128)(2,1)} async-done(((bf16[8,16,2,256]{3,1,0,2:T(8,128)(2,1)}), bf16[8,256,2,256]{3,1,0,2:T(8,128)(2,1)}) %all-gather.4.cloned.1.call-update) | async-done | bytes 2097168 | tf_op jit(solution)/shard_map/all_gather | solution.py:127
  195.2 3.1 fusion.75
  198.3 2.3 copy.46
  200.6 2.3 copy.47
  202.9 2.4 fusion.79
  205.3 52.1 %all-gather.8.cloned.1.call-done = bf16[8,16,16,2,256]{4,2,3,0,1:T(8,128)(2,1)} async-done(((bf16[8,1,16,2,256]{4,2,3,0,1:T(8,128)(2,1)}), bf16[8,16,16,2,256]{4,2,3,0,1:T(8,128)(2,1)}) %all-gather.8.cloned.1.call-update) | async-done | bytes 2097168 | tf_op jit(solution)/shard_map/all_gather | solution.py:139
  257.4 2.8 fusion.76
  260.1 1.1 copy.60
  261.2 4.4 %reshape_squeeze.22 = bf16[8,256,4,64]{3,2,1,0:T(4,128)(2,1)} reshape(bf16[8,16,16,1,256]{4,2,1,0,3:T(8,128)(2,1)} %copy.60) | data formatting | bytes 2097152 | tf_op jit(solution)/shard_map/reshape;squeeze | solution.py:147
  265.7 2.3 copy.61
  267.9 4.4 %reshape_squeeze.23 = bf16[8,256,4,64]{3,2,1,0:T(4,128)(2,1)} reshape(bf16[8,16,16,1,256]{4,2,1,0,3:T(8,128)(2,1)} %copy.61) | data formatting | bytes 2097152 | tf_op jit(solution)/shard_map/reshape;squeeze | solution.py:146
  272.4 2.7 fusion.81
  275.5 1.0 copy-done.1
  276.6 0.9 fusion.38
  278.3 1.6 fusion.47
  279.9 1.0 slice.99
  281.0 1.0 slice.100
  282.1 88.5 %all-reduce.6.cloned.1.call-done = (f32[8,13,1920]{2,1,0:T(8,128)}, f32[8,16,1920]{2,1,0:T(8,128)}) async-done(((f32[8,13,1920]{2,1,0:T(8,128)}, f32[8,16,1920]{2,1,0:T(8,128)}), (f32[8,13,1920]{2,1,0:T(8,128)}, f32[8,16,1920]{2,1,0:T(8,128)})) %all-reduce.6.cloned.1.call-update) | async-done | bytes 1781776 | tf_op jit(solution)/shard_map/psum | solution.py:160
  370.6 1.4 fusion.59
  372.0 0.8 copy.66
  372.8 0.9 fusion.60
  (90 shorter events, 9.3 us)
Async XLA Ops:
  7.2 1.8 copy-start
  7.2 3.7 copy-start.14
  7.2 3.9 %copy-start.9 = (f32[4096,32]{0,1:T(8,128)S(1)}, f32[4096,32]{0,1:T(8,128)}, u32[]{:S(2)}) copy-start(f32[4096,32]{0,1:T(8,128)} %param.19) | copy-start | bytes 1572868
  7.2 54.0 %all-reduce.4.cloned.1.call-start = ((), (), s32[]{:S(2)}) async-start(), calls=%async_computation | async-start | bytes 184320 | tf_op jit(solution)/shard_map/psum | solution.py:70
  10.9 122.5 %all-gather.6.cloned.1.call-start = ((), (), s32[]{:S(2)}) async-start(), calls=%async_computation.2 | async-start | bytes 1810432 | tf_op jit(solution)/shard_map/all_gather | solution.py:138
  14.0 7.4 %copy-start.13 = (bf16[1,16,1920]{2,1,0:T(8,128)(2,1)S(1)}, bf16[1,16,1920]{2,1,0:T(8,128)(2,1)}, u32[]{:S(2)}) copy-start(bf16[1,16,1920]{2,1,0:T(8,128)(2,1)} %param.23) | copy-start | bytes 184324
  19.3 5.9 %copy-start.16 = (f32[16,13,1]{1,0,2:T(8,128)S(1)}, f32[16,13,1]{1,0,2:T(8,128)}, u32[]{:S(2)}) copy-start(f32[16,13,1]{1,0,2:T(8,128)} %constant.46) | copy-start | bytes 2500
  19.3 6.1 %copy-start.15 = (f32[1920]{0:T(1024)S(1)}, f32[1920]{0:T(1024)}, u32[]{:S(2)}) copy-start(f32[1920]{0:T(1024)} %param.22) | copy-start | bytes 23044
  27.4 0.8 copy-start.2
  66.0 1.2 copy-start.3
  66.0 2.1 copy-start.17
  67.2 0.7 copy-start.6
  67.9 4.1 %copy-start.11 = (bf16[8,16,2,256]{3,2,1,0:T(2,128)(2,1)S(1)}, bf16[8,16,2,256]{3,2,1,0:T(2,128)(2,1)}, u32[]{:S(2)}) copy-start(bf16[8,16,2,256]{3,2,1,0:T(2,128)(2,1)} %param.15) | copy-start | bytes 393220
  70.4 0.7 copy-start.7
  72.0 123.3 %all-gather.4.cloned.1.call-start = ((), (), s32[]{:S(2)}) async-start(), calls=%async_computation.1 | async-start | bytes 2228224 | tf_op jit(solution)/shard_map/all_gather | solution.py:127
  78.4 179.0 %all-gather.8.cloned.1.call-start = ((), (), s32[]{:S(2)}) async-start(), calls=%async_computation.3 | async-start | bytes 2228224 | tf_op jit(solution)/shard_map/all_gather | solution.py:139
  81.5 289.1 %all-reduce.6.cloned.1.call-start = ((), (), s32[]{:S(2)}) async-start(), calls=%async_computation.4 | async-start | bytes 3932160 | tf_op jit(solution)/shard_map/psum | solution.py:160
  136.1 7.5 %copy-start.12 = (bf16[8,29,4,64]{3,1,2,0:T(8,128)(2,1)S(1)}, bf16[8,29,4,64]{3,1,2,0:T(8,128)(2,1)}, u32[]{:S(2)}) copy-start(bf16[8,29,4,64]{3,1,2,0:T(8,128)(2,1)} %get-tuple-element.18) | copy-start | bytes 356356
  272.4 2.7 copy-start.4
  275.0 1.5 copy-start.1
  275.0 1.5 copy-start.10
  275.4 2.1 copy-start.5
  275.5 2.1 copy-start.18
  370.6 2.2 copy-start.8
Sparse Core Ops, SparseCore 0:
  11.0 50.2 all-reduce.3
  72.1 61.2 all-gather.5
  136.3 58.9 all-gather.3
  198.8 58.5 all-gather.7
  282.2 88.3 all-reduce.5
where the time goes:
time: 381 us; the launch traced here: 380 us
  waiting for transfers between devices  268 us (70%)
  local copies, waits for them, and re-layouts  64.1 us (17%)
  matrix products  21.8 us (6%)
  between operations  14.2 us (4%)
  other arithmetic  11.7 us (3%)
    psum x1, waiting for transfers between devices, body(): lax.psum((partial_small, partial_large), 'head')  88.5 us
    all_gather x1, waiting for transfers between devices, body(): large_piece = lax.all_gather(fine_large, 'seq', axis=1, tiled=True)  52.1 us
    all_gather x1, waiting for transfers between devices, body(): small_piece = lax.all_gather(fine_small, 'seq', axis=1, tiled=True)  51.4 us
    all_gather x1, waiting for transfers between devices, body(): pieces = lax.all_gather(coarse_local, 'seq', axis=1, tiled=True)  48.1 us
    psum x1, waiting for transfers between devices, body(): lax.psum(partial_rows.astype(jnp.bfloat16), 'head').astype(jnp.float32)  27.8 us
    unnamed x43, local copies, waits for them, and re-layouts  14.5 us
    dot_general x3, matrix products, accumulate(): jnp.einsum('bqhe,bkhe->bqhk', queries, keys, preferred_element_type=jnp.f...  8.52 us
  transfers between devices with their start and end apart: 5, of which 5 were waited for; matrix products, arithmetic and copies ran while one was open for 15% of the time, Pallas kernels for 0%

commit v1 on v0

v1 whole, which is shorter than its diff:
```python
import functools

import jax
import jax.numpy as jnp
from jax import lax
from jax.experimental import pallas as pl
from jax.experimental.pallas import tpu as pltpu
from jax.sharding import PartitionSpec as P

MESH = pl.DeviceIdType.MESH
S13 = 13
S16 = 16
D = 1920
W = 256
IMG = 8
HALF = 8
HEADSETS = 4
DPS = 4
TOK = 32
LARGE = IMG * S16
SMALL = IMG * S13
ROWS = 240
WIDE = 1024
SECOND = D - WIDE
F32 = jnp.float32
BF16 = jnp.bfloat16
VMEM_LIMIT = 58 * 1024 * 1024


def dot(a, b):
    return jnp.dot(a, b, preferred_element_type=F32)


def dot_nt(a, b):
    return lax.dot_general(a, b, (((1,), (1,)), ((), ())), preferred_element_type=F32)


def iota(shape, axis):
    return lax.broadcasted_iota(jnp.int32, shape, axis)


def flags(condition):
    return jnp.where(condition, 1.0, 0.0).astype(BF16)


def split(x):
    high = x.astype(BF16)
    return high, (x - high.astype(F32)).astype(BF16)


def layer_norm(x):
    centred = x - jnp.mean(x, axis=-1, keepdims=True)
    variance = jnp.mean(centred * centred, axis=-1, keepdims=True)
    return centred * lax.rsqrt(variance + 1e-06)


def remote(src, dst, send, recv, **device):
    return pltpu.make_async_remote_copy(
        src_ref=src, dst_ref=dst, send_sem=send, recv_sem=recv, device_id=device, device_id_type=MESH
    )


def kernel(
    labels, head_scale, ids, cache, feature_sum, bias, position,
    thirteen_hbm, table_hbm, codebook_hbm, embed_hbm, qkv_hbm, out_hbm,
    o13, o16,
    thirteen, table, codebook, embed, qkv, wout,
    cache_send, cache_recv, mod_a, mod_b, mod, feats, xhat, xmod,
    qkv_send, own_recv, other_recv, weights, vext, att_send, att_recv, att_all,
    local_sem,
    ma_s, ma_r, mb_s, mb_r, ca_s, ca_r, own_s, own_r, oth_s, oth_r, att_s, att_r,
    wz_s, wz_r, wy_s, wy_r, wx_s, wx_r, wc_s, wc_r,
):
    x = lax.axis_index("dp")
    seq = lax.axis_index("seq")
    h = lax.axis_index("head")
    zh, u = seq // HALF, seq % HALF
    y, core = u // 2, u % 2
    me = h * HALF + u

    def in_half(place):
        return zh * HALF + place

    def in_other(place):
        return (1 - zh) * HALF + place

    col0 = pl.multiple_of(u * W - (u // 7) * 128, 128)
    loads = [
        (table_hbm.at[:, :, pl.ds(col0, W)], table),
        (codebook_hbm, codebook),
        (embed_hbm, embed),
        (thirteen_hbm, thirteen),
        (out_hbm.at[:, pl.ds(0, WIDE)], wout.at[0, pl.ds(pl.multiple_of(h * W, W), W), :]),
        (out_hbm.at[:, pl.ds(SECOND, WIDE)], wout.at[1, pl.ds(pl.multiple_of(h * W, W), W), :]),
        (qkv_hbm, qkv),
    ]
    loads = [pltpu.make_async_copy(a, b, local_sem.at[i]) for i, (a, b) in enumerate(loads)]
    for load in loads:
        load.start()

    barrier = pltpu.get_barrier_semaphore()

    def greet_half(d, c):
        p = (me + d) % (HEADSETS * HALF)
        pl.semaphore_signal(
            barrier, inc=1, device_id={"seq": in_half(p % HALF), "head": p // HALF}, device_id_type=MESH
        )
        return c

    def greet_other(d, c):
        pl.semaphore_signal(
            barrier, inc=1, device_id={"seq": in_other((u + d) % HALF)}, device_id_type=MESH
        )
        return c

    def greet_dp(d, c):
        pl.semaphore_signal(barrier, inc=1, device_id={"dp": (x + d) % DPS}, device_id_type=MESH)
        return c

    lax.fori_loop(1, HEADSETS * HALF, greet_half, 0)
    lax.fori_loop(0, HALF, greet_other, 0)
    lax.fori_loop(1, DPS, greet_dp, 0)

    group = flags((iota((W, W), 0) >> 6) == (iota((W, W), 1) >> 6))

    def normalize(v):
        high, low = split(v * v)
        return v * lax.rsqrt(dot(high, group) + dot(low, group) + 1e-06)

    keys = cache[:, 0:16, :].reshape(IMG * 16, W).astype(F32)
    cache_send[:, 0:16, :] = normalize(keys).astype(BF16).reshape(IMG, 16, W)
    cache_send[:, 16:32, :] = cache[:, 16:32, :]

    loads[0].wait()
    owned = table.shape[1]
    rows8 = iota((IMG, owned), 0)
    wanted = jnp.zeros((IMG, owned), jnp.int32)
    for b in range(IMG):
        wanted = jnp.where(rows8 == b, labels[b] - h * owned, wanted)
    onehot = flags(wanted == iota((IMG, owned), 1))
    parts = [dot(onehot, table[t]) for t in range(3)] + [jnp.zeros((IMG, W), F32)]
    mod_a[h] = jnp.concatenate(parts, axis=0).astype(BF16)

    pl.semaphore_wait(barrier, HEADSETS * HALF - 1 + HALF + DPS - 1)

    def mod_a_copy(d):
        to = (h + d) % HEADSETS
        return remote(mod_a.at[h], mod_a.at[h], ma_s.at[to], ma_r.at[h], head=to)

    def mod_b_copy(d):
        to = (u + d) % HALF
        return remote(mod_b.at[u], mod_b.at[u], mb_s.at[to], mb_r.at[u], seq=in_half(to))

    def cache_copy(d):
        to = (seq + d) % 16
        return remote(cache_send.at[to % HALF], cache_recv.at[seq], ca_s.at[to], ca_r.at[seq], seq=to)

    def own_copy(d):
        to = (u + d) % HALF
        return remote(qkv_send.at[to], own_recv.at[u], own_s.at[to], own_r.at[u], seq=in_half(to))

    def other_copy(d):
        to = (u + d) % HALF
        return remote(
            qkv_send.at[to, pl.ds(TOK, 2 * TOK), :], other_recv.at[u], oth_s.at[to], oth_r.at[u],
            seq=in_other(to),
        )

    def att_copy(d):
        p = (me + d) % (HEADSETS * HALF)
        return remote(
            att_send.at[p % HALF], att_recv.at[h, u], att_s.at[p], att_r.at[me],
            seq=in_half(p % HALF), head=p // HALF,
        )

    def piece(part, start, count):
        return wout.at[core, pl.ds(pl.multiple_of(part * W + start, 16), count), :]

    def wz_copy(d):
        to = (h + d) % HEADSETS
        ref = piece(h, x * 64 + y * 16, 16)
        return remote(ref, ref, wz_s.at[to], wz_r.at[h], head=to)

    def wy_copy(i):
        to, part = (y + 1 + i // 3) % 4, (h + 1 + i % 3) % HEADSETS
        ref = piece(part, x * 64 + y * 16, 16)
        return remote(
            ref, ref, wy_s.at[to * 4 + part], wy_r.at[y * 4 + part], seq=in_half(to * 2 + core)
        )

    def wx_copy(i):
        to, part = (x + 1 + i // 3) % DPS, (h + 1 + i % 3) % HEADSETS
        ref = piece(part, x * 64, 64)
        return remote(ref, ref, wx_s.at[to * 4 + part], wx_r.at[x * 4 + part], dp=to)

    def wc_copy(i):
        part = (h + 1 + i) % HEADSETS
        ref = piece(part, 0, W)
        return remote(ref, ref, wc_s.at[part], wc_r.at[part], seq=in_half(u + 1 - 2 * core))

    def each(low, high, copy, action):
        def step(d, c):
            getattr(copy(d), action)()
            return c

        lax.fori_loop(low, high, step, 0)

    def arrived(low, high, ref_of, sem_of):
        def step(d, c):
            ref, sem = ref_of(d), sem_of(d)
            remote(ref, ref, ma_s.at[0], sem, head=(h + 1) % HEADSETS).wait_recv()
            return c

        lax.fori_loop(low, high, step, 0)

    each(1, HEADSETS, mod_a_copy, "start")
    loads[4].wait()
    loads[5].wait()
    each(1, HEADSETS, wz_copy, "start")
    each(1, 16, cache_copy, "start")
    cache_recv[seq] = cache_send[u]

    loads[1].wait()
    place = 26 * seq - 3 + 3 * ((16 - seq) // 16)
    lower = place // 32
    upper = lower + 1 - lower // (S13 - 1)
    weight = (place % 32).astype(F32) * (1.0 / 32.0)
    low_ids, high_ids = ids[lower], ids[upper]
    span = 512

    def look(c, total):
        start = pl.multiple_of(c * span, span)
        entry = iota((IMG, span), 1) + c * span
        hits = []
        for j in range(S13):
            hits.append(
                jnp.where(low_ids[:, j : j + 1] == entry, 1.0 - weight, 0.0)
                + jnp.where(high_ids[:, j : j + 1] == entry, weight, 0.0)
            )
        hits.append(jnp.zeros((IMG, span), F32))
        hits = jnp.concatenate(hits, axis=0).astype(BF16)
        high, low = split(codebook[:, pl.ds(start, span)])
        return total + dot_nt(hits, high) + dot_nt(hits, low)

    looked = lax.fori_loop(0, codebook.shape[1] // span, look, jnp.zeros((SMALL + IMG, 32), F32))
    for s in range(S16):
        at = max(26 * s - 3, 0)
        low = at // 32
        up = min(low + 1, S13 - 1)
        frac = (at % 32) / 32.0
        feats[s * IMG : (s + 1) * IMG, :] = (
            feature_sum[:, s * 32 : (s + 1) * 32]
            + looked[low * IMG : (low + 1) * IMG] * (1.0 - frac)
            + looked[up * IMG : (up + 1) * IMG] * frac
        )

    arrived(1, HEADSETS, lambda d: mod_a.at[(h + d) % HEADSETS], lambda d: ma_r.at[(h + d) % HEADSETS])
    total = mod_a[0].astype(F32)
    for part in range(1, HEADSETS):
        total = total + mod_a[part].astype(F32)
    mod_b[u] = total.astype(BF16)
    each(1, HALF, mod_b_copy, "start")

    loads[2].wait()
    feats_high, feats_low = split(feats[...])
    embed_high, embed_low = split(embed[...])
    xhat[0:LARGE, :] = dot(feats_high, embed_high) + dot(feats_high, embed_low) + dot(feats_low, embed_high)

    arrived(
        1, HEADSETS,
        lambda d: piece((h + d) % HEADSETS, x * 64 + y * 16, 16),
        lambda d: wz_r.at[(h + d) % HEADSETS],
    )
    each(0, 9, wy_copy, "start")

    for i in range(S16 // 2):
        table_rows = position[2 * i : 2 * i + 2, :].astype(F32)
        both = jnp.concatenate([jnp.broadcast_to(table_rows[k : k + 1], (IMG, D)) for k in range(2)], axis=0)
        rows = xhat[16 * i : 16 * i + 16, :] + bias[...] + both
        xhat[16 * i : 16 * i + 16, :] = layer_norm(rows.astype(BF16).astype(F32))
    loads[3].wait()
    for i in range(SMALL // 16):
        xhat[LARGE + 16 * i : LARGE + 16 * i + 16, :] = layer_norm(thirteen[16 * i : 16 * i + 16, :].astype(F32))
    xhat[LARGE + SMALL - 8 : LARGE + SMALL, :] = layer_norm(thirteen[SMALL - 8 : SMALL, :].astype(F32))
    xhat[LARGE + SMALL : ROWS, :] = jnp.zeros((ROWS - LARGE - SMALL, D), F32)

    arrived(1, HALF, lambda d: mod_b.at[(u + d) % HALF], lambda d: mb_r.at[(u + d) % HALF])
    for c in range(HALF):
        chunk = mod_b[c].astype(F32)
        if c == HALF - 1:
            chunk = chunk[:, 128:]
        width = chunk.shape[1]
        mod[0, :, c * W : c * W + width] = chunk[0:8]
        mod[1, :, c * W : c * W + width] = 1.0 + chunk[8:16]
        mod[2, :, c * W : c * W + width] = chunk[16:24]

    def modulate(i, carry):
        at = pl.multiple_of(i * 16, 16)
        rows = xhat[pl.ds(at, 16), :].reshape(2, IMG, D)
        rows = rows * mod[1][None] + mod[0][None]
        xmod[pl.ds(at, 16), :] = rows.reshape(16, D).astype(BF16)
        return carry

    lax.fori_loop(0, ROWS // 16, modulate, 0)

    loads[6].wait()
    r, c = iota((IMG * TOK, ROWS), 0), iota((IMG * TOK, ROWS), 1)
    token = r & (TOK - 1)
    to_image = flags((token < S13 + S16) & (c == token * IMG + (r >> 5)))
    lane_head = iota((1, W), 1) >> 6
    scales = jnp.zeros((1, W), F32)
    for k in range(4):
        scales = jnp.where(lane_head == k, head_scale[k], scales)
    for t in range(3):
        projected = dot(xmod[...], qkv[t])
        if t == 0:
            projected = normalize(projected) * scales
        elif t == 1:
            projected = normalize(projected)
        moved = dot(to_image, projected.astype(BF16)).astype(BF16)
        qkv_send[:, t * TOK : (t + 1) * TOK, :] = moved.reshape(IMG, TOK, W)
    each(0, HALF, other_copy, "start")
    each(1, HALF, own_copy, "start")
    own_recv[u] = qkv_send[u]

    def y_place(i):
        return (y + 1 + i // 3) % 4, (h + 1 + i % 3) % HEADSETS

    arrived(
        0, 9,
        lambda i: piece(y_place(i)[1], x * 64 + y_place(i)[0] * 16, 16),
        lambda i: wy_r.at[y_place(i)[0] * 4 + y_place(i)[1]],
    )
    each(0, 9, wx_copy, "start")

    arrived(1, 16, lambda d: cache_recv.at[(seq + d) % 16], lambda d: ca_r.at[(seq + d) % 16])
    arrived(1, HALF, lambda d: own_recv.at[(u + d) % HALF], lambda d: own_r.at[(u + d) % HALF])
    lanes = iota((W, W), 1) >> 6
    key = iota((W, W), 0)
    queries = own_recv[:, 0:TOK, :].reshape(W, W)
    masked = [jnp.where(lanes == k, queries, jnp.zeros_like(queries)) for k in range(4)]
    seen = jnp.where((iota((W, W), 0) & 31) >= S16, jnp.where((iota((W, W), 1) & 31) < S16, 0.0, 1.0), 1.0)

    def part(index, keys, values, valid, fine):
        for k in range(4):
            column = (index * 4 + k) * W
            scores = jnp.exp(dot_nt(masked[k], keys))
            if fine:
                scores = scores * seen
            weights[:, column : column + W] = scores.astype(BF16)
            use = valid & (lanes == k)
            vext[column : column + W, 0:W] = jnp.where(use, values, jnp.zeros_like(values))
            vext[column : column + W, W : 2 * W] = flags(use)

    def fine_valid(half):
        tok = key & 31
        return (tok < S16) | ((tok < S16 + S13) & (half * HALF + (key >> 5) < S13))

    part(
        0, cache_recv[:, 0:16, :].reshape(W, W), cache_recv[:, 16:32, :].reshape(W, W), key < W - 1, False
    )
    part(
        1, own_recv[:, TOK : 2 * TOK, :].reshape(W, W), own_recv[:, 2 * TOK : 3 * TOK, :].reshape(W, W),
        fine_valid(zh), True,
    )
    arrived(0, HALF, lambda d: other_recv.at[(u + d) % HALF], lambda d: oth_r.at[(u + d) % HALF])
    part(
        2, other_recv[:, 0:TOK, :].reshape(W, W), other_recv[:, TOK : 2 * TOK, :].reshape(W, W),
        fine_valid(1 - zh), True,
    )
    sums = dot(weights[...], vext[...])
    attended = (sums[:, 0:W] / sums[:, W : 2 * W]).astype(BF16)
    att_send[...] = attended.reshape(HALF, TOK, W)
    each(1, HEADSETS * HALF, att_copy, "start")
    att_recv[h, u] = att_send[u]

    def x_place(i):
        return (x + 1 + i // 3) % DPS, (h + 1 + i % 3) % HEADSETS

    arrived(
        0, 9,
        lambda i: piece(x_place(i)[1], x_place(i)[0] * 64, 64),
        lambda i: wx_r.at[x_place(i)[0] * 4 + x_place(i)[1]],
    )
    each(0, 3, wc_copy, "start")

    r, c = iota((ROWS, W), 0), iota((ROWS, W), 1)
    small = r - LARGE
    source = jnp.where(r < LARGE, (r >> 4) * TOK + (r & 15), (small & 7) * TOK + S16 + (small >> 3))
    to_row = flags(c == source)
    arrived(
        1, HEADSETS * HALF,
        lambda d: att_recv.at[((me + d) % (HEADSETS * HALF)) // HALF, (me + d) % HALF],
        lambda d: att_r.at[(me + d) % (HEADSETS * HALF)],
    )
    for k in range(HEADSETS):
        att_all[:, k * W : (k + 1) * W] = dot(to_row, att_recv[k].reshape(W, W)).astype(BF16)
    arrived(
        0, 3,
        lambda i: wout.at[1 - core, pl.ds(pl.multiple_of(((h + 1 + i) % HEADSETS) * W, W), W), :],
        lambda i: wc_r.at[(h + 1 + i) % HEADSETS],
    )
    kept = seq < S13
    for start in range(0, D, W):
        width = min(W, D - start)
        side = 0 if start < WIDE else 1
        first = start - side * SECOND
        branch = dot(att_all[...], wout[side, :, first : first + width])
        gate = mod[2, :, start : start + width]
        for b in range(IMG):
            o16[b, :, start : start + width] = (gate[b : b + 1] * branch[b * S16 : (b + 1) * S16]).astype(BF16)
        for j in range(S13):
            rows = gate * branch[LARGE + j * IMG : LARGE + (j + 1) * IMG]
            o13[j, :, start : start + width] = jnp.where(kept, rows, jnp.zeros_like(rows)).astype(BF16)

    each(1, HEADSETS, mod_a_copy, "wait_send")
    each(1, HALF, mod_b_copy, "wait_send")
    each(1, 16, cache_copy, "wait_send")
    each(1, HALF, own_copy, "wait_send")
    each(0, HALF, other_copy, "wait_send")
    each(1, HEADSETS * HALF, att_copy, "wait_send")
    each(1, HEADSETS, wz_copy, "wait_send")
    each(0, 9, wy_copy, "wait_send")
    each(0, 9, wx_copy, "wait_send")
    each(0, 3, wc_copy, "wait_send")


def body(
    map_thirteen, kv_cache, class_labels, class_table, sampled_ids, codebook, feature_sum,
    embed_weight, embed_bias, position_table, qkv_weight, out_weight, head_scale,
):
    owned = class_table.shape[0]
    vocabulary = codebook.shape[0]
    vmem = pl.BlockSpec(memory_space=pltpu.VMEM)
    smem = pl.BlockSpec(memory_space=pltpu.SMEM)
    anywhere = pl.BlockSpec(memory_space=pl.ANY)
    dma = pltpu.SemaphoreType.DMA
    o13, o16 = pl.pallas_call(
        kernel,
        out_shape=(
            jax.ShapeDtypeStruct((S13, IMG, D), BF16),
            jax.ShapeDtypeStruct((IMG, S16, D), BF16),
        ),
        in_specs=[smem, smem, vmem, vmem, vmem, vmem, vmem] + [anywhere] * 6,
        out_specs=(vmem, vmem),
        scratch_shapes=[
            pltpu.VMEM((SMALL, D), BF16),
            pltpu.VMEM((3, owned, W), BF16),
            pltpu.VMEM((32, vocabulary), F32),
            pltpu.VMEM((32, D), F32),
            pltpu.VMEM((3, D, W), BF16),
            pltpu.VMEM((2, HEADSETS * W, WIDE), BF16),
            pltpu.VMEM((IMG, 32, W), BF16),
            pltpu.VMEM((16, 32, W), BF16),
            pltpu.VMEM((HEADSETS, 32, W), BF16),
            pltpu.VMEM((HALF, 32, W), BF16),
            pltpu.VMEM((3, IMG, D), F32),
            pltpu.VMEM((LARGE, 32), F32),
            pltpu.VMEM((ROWS, D), F32),
            pltpu.VMEM((ROWS, D), BF16),
            pltpu.VMEM((IMG, 3 * TOK, W), BF16),
            pltpu.VMEM((HALF, 3 * TOK, W), BF16),
            pltpu.VMEM((HALF, 2 * TOK, W), BF16),
            pltpu.VMEM((W, 12 * W), BF16),
            pltpu.VMEM((12 * W, 2 * W), BF16),
            pltpu.VMEM((HALF, TOK, W), BF16),
            pltpu.VMEM((HEADSETS, HALF, TOK, W), BF16),
            pltpu.VMEM((ROWS, HEADSETS * W), BF16),
            dma((8,)),
        ]
        + [dma((n,)) for n in (4, 4, 8, 8, 16, 16, 8, 8, 8, 8, 32, 32, 4, 4, 16, 16, 16, 16, 4, 4)],
        compiler_params=pltpu.CompilerParams(
            collective_id=0, has_side_effects=True, vmem_limit_bytes=VMEM_LIMIT
        ),
        cost_estimate=pl.CostEstimate(flops=3_000_000_000, bytes_accessed=12_000_000, transcendentals=1_000_000),
    )(
        class_labels,
        head_scale,
        sampled_ids.transpose(1, 0, 2),
        kv_cache.transpose(0, 2, 1, 3).reshape(IMG, 32, W),
        feature_sum.reshape(IMG, S16 * 32),
        embed_bias.reshape(1, D),
        position_table.reshape(S16, D),
        map_thirteen.reshape(IMG, S13, D).transpose(1, 0, 2).reshape(SMALL, D),
        class_table.transpose(1, 0, 2),
        codebook.T,
        embed_weight,
        qkv_weight.transpose(1, 0, 2),
        out_weight,
    )
    return o13.transpose(1, 0, 2)[:, None], o16[:, None]


def solution(mesh):
    placed = (
        P("dp", "seq", None, None),
        P("dp", "seq", None, "head"),
        P("dp"),
        P("head", None, None),
        P("dp", None, None),
        P(),
        P("dp", "seq", None),
        P(),
        P(),
        P("seq", None, None),
        P(None, None, "head"),
        P("head", None),
        P("head"),
    )
    return jax.shard_map(
        body,
        mesh=mesh,
        in_specs=placed,
        out_specs=(P("dp", "seq", None, None), P("dp", "seq", None, None)),
        check_vma=False,
    )
```

time: 381 us -> 67.6 us (0.18)
  the two profiles are of different devices: /device:TPU:1 before, /device:TPU:255 now
where the time goes in v1:
time: 67.6 us; the launch traced here: 67.3 us
  Pallas kernels  58.9 us (87%)
  local copies, waits for them, and re-layouts  7.81 us (12%)
    pallas_call x1, Pallas kernels, body(): pl.pallas_call(kernel, out_shape=(jax.ShapeDtypeStruct((S13, IMG, D), BF1...  58.9 us
    unnamed x3, local copies, waits for them, and re-layouts  4.94 us
    transpose x1, local copies, waits for them, and re-layouts, body(): kv_cache.transpose(0, 2, 1, 3).reshape(IMG, 32, W)  1.57 us

profile of v1, /device:TPU:255, one launch (start us, length us, event | category | flops | bytes accessed | tf_op | source)
XLA Modules:
  0.0 67.3 jit_solution(6898488380382385069)
XLA Ops:
  0.6 1.3 %reshape.24.bias = f32[1,1920]{1,0:T(1,128)} reshape(f32[1920]{0:T(1024)} %param.21) | data formatting | bytes 15360 | tf_op jit(solution)/shard_map/reshape | solution.py:482
  1.9 1.3 %copy.19 = f32[8,1,512]{2,0,1:T(8,128)} copy(f32[8,1,512]{2,1,0:T(1,128)} %param.19) | data formatting | bytes 32768
  3.2 1.6 %copy.15 = bf16[8,2,16,256]{3,2,1,0:T(8,128)(2,1)} copy(bf16[8,2,16,256]{3,1,2,0:T(2,128)(2,1)} %bitcast.23) | data formatting | bytes 262144 | tf_op jit(solution)/shard_map/transpose | solution.py:480
  4.8 58.9 %shard_map.140 = (bf16[13,8,1920]{2,1,0:T(8,128)(2,1)}, bf16[8,16,1920]{2,1,0:T(8,128)(2,1)}) custom-call(s32[8]{0:T(128)} %labels.1, f32[4]{0:T(128)} %head_scale.1, s32[13,8,13]{2,1,0:T(8,128)} %bitcast.31, bf16[8,32,256]{2,1,0:T(8,128)(2,1)} %bitcast.24, f32[8,512]{1,0:T(8,128)} %bitcast.25, f32[1,1920]{1,0:T(1,128)} %reshape.24.bias, ...), custom_call_target="tpu_custom_call" | custom-call | flops 3000000000 | bytes 12000000 | tf_op jit(solution)/shard_map/pallas_call | solution.py:438
  63.7 1.8 %copy.22 = bf16[8,1,13,1920]{3,0,2,1:T(8,128)(2,1)} copy(bf16[8,1,13,1920]{3,0,2,1:T(8,128)(2,1)} %bitcast.22) | data formatting | bytes 798720
  65.5 1.8 %copy.23 = bf16[8,1,16,1920]{3,2,1,0:T(8,128)(2,1)} copy(bf16[8,1,16,1920]{3,2,1,0:T(8,128)(2,1)} %bitcast.21) | data formatting | bytes 983040

commit v2 on v1

v2 whole, which is shorter than its diff:
```python
import functools

import jax
import jax.numpy as jnp
from jax import lax
from jax.experimental import pallas as pl
from jax.experimental.pallas import tpu as pltpu
from jax.sharding import PartitionSpec as P

MESH = pl.DeviceIdType.MESH
S13 = 13
S16 = 16
D = 1920
W = 256
IMG = 8
HALF = 8
HEADSETS = 4
DPS = 4
TOK = 16
LARGE = IMG * S16
SMALL = IMG * S13
PADDED = SMALL + IMG
ROWS = 2 * LARGE + PADDED
SPAN = 512
WIDE = 1024
SECOND = D - WIDE
F32 = jnp.float32
BF16 = jnp.bfloat16
VMEM_LIMIT = 58 * 1024 * 1024


def dot(a, b):
    return jnp.dot(a, b, preferred_element_type=F32)


def dot_nt(a, b):
    return lax.dot_general(a, b, (((1,), (1,)), ((), ())), preferred_element_type=F32)


def iota(shape, axis):
    return lax.broadcasted_iota(jnp.int32, shape, axis)


def flags(condition):
    return jnp.where(condition, 1.0, 0.0).astype(BF16)


def split(x):
    high = x.astype(BF16)
    return high, (x - high.astype(F32)).astype(BF16)


def layer_norm(x):
    centred = x - jnp.mean(x, axis=-1, keepdims=True)
    variance = jnp.mean(centred * centred, axis=-1, keepdims=True)
    return centred * lax.rsqrt(variance + 1e-06)


def remote(src, dst, send, recv, **device):
    return pltpu.make_async_remote_copy(
        src_ref=src, dst_ref=dst, send_sem=send, recv_sem=recv, device_id=device, device_id_type=MESH
    )


def kernel(
    labels, head_scale, ids, cache, feature_sum, bias, position,
    thirteen_hbm, table_hbm, codebook_hbm, embed_hbm, qkv_hbm, out_hbm,
    o13, o16,
    thirteen, table, codebook, embed, qkv, wout,
    cache_send, cache_recv, mod_a, mod_b, mod, far_position, far_features, id_lanes, xhat, xmod,
    small_send, small_near, small_far, large_send, large_near,
    weights, vext, att_small, att_large, small_recv, large_recv, small_all, large_all,
    local_sem,
    ma_s, ma_r, mb_s, mb_r, fp_s, fp_r, ca_s, ca_r, sn_s, sn_r, sf_s, sf_r, ln_s, ln_r,
    as_s, as_r, al_s, al_r, wz_s, wz_r, wy_s, wy_r, wx_s, wx_r, wc_s, wc_r,
):
    x = lax.axis_index("dp")
    seq = lax.axis_index("seq")
    h = lax.axis_index("head")
    zh, u = seq // HALF, seq % HALF
    y, core = u // 2, u % 2
    me = h * HALF + u

    def in_half(place):
        return zh * HALF + place

    def in_other(place):
        return (1 - zh) * HALF + place

    col0 = pl.multiple_of(u * W - (u // 7) * 128, 128)
    loads = [
        (table_hbm.at[:, :, pl.ds(col0, W)], table),
        (codebook_hbm, codebook),
        (embed_hbm, embed),
        (thirteen_hbm, thirteen),
        (out_hbm.at[:, pl.ds(0, WIDE)], wout.at[0, pl.ds(pl.multiple_of(h * W, W), W), :]),
        (out_hbm.at[:, pl.ds(SECOND, WIDE)], wout.at[1, pl.ds(pl.multiple_of(h * W, W), W), :]),
        (qkv_hbm, qkv),
    ]
    loads = [pltpu.make_async_copy(a, b, local_sem.at[i]) for i, (a, b) in enumerate(loads)]
    for load in loads:
        load.start()

    barrier = pltpu.get_barrier_semaphore()

    def greet_half(d, c):
        p = (me + d) % (HEADSETS * HALF)
        pl.semaphore_signal(
            barrier, inc=1, device_id={"seq": in_half(p % HALF), "head": p // HALF}, device_id_type=MESH
        )
        return c

    def greet_other(d, c):
        pl.semaphore_signal(
            barrier, inc=1, device_id={"seq": in_other((u + d) % HALF)}, device_id_type=MESH
        )
        return c

    def greet_dp(d, c):
        pl.semaphore_signal(barrier, inc=1, device_id={"dp": (x + d) % DPS}, device_id_type=MESH)
        return c

    lax.fori_loop(1, HEADSETS * HALF, greet_half, 0)
    lax.fori_loop(0, HALF, greet_other, 0)
    lax.fori_loop(1, DPS, greet_dp, 0)

    def mod_a_copy(d):
        to = (h + d) % HEADSETS
        return remote(mod_a.at[h], mod_a.at[h], ma_s.at[to], ma_r.at[h], head=to)

    def mod_b_copy(d):
        to = (u + d) % HALF
        return remote(mod_b.at[u], mod_b.at[u], mb_s.at[to], mb_r.at[u], seq=in_half(to))

    def cache_copy(d):
        to = (seq + d) % 16
        return remote(cache_send.at[to % HALF], cache_recv.at[seq], ca_s.at[to], ca_r.at[seq], seq=to)

    def small_near_copy(d):
        to = (u + d) % HALF
        return remote(small_send.at[to], small_near.at[u], sn_s.at[to], sn_r.at[u], seq=in_half(to))

    def small_far_copy(d):
        to = (u + d) % HALF
        return remote(
            small_send.at[to, pl.ds(TOK, 2 * TOK), :], small_far.at[u], sf_s.at[to], sf_r.at[u],
            seq=in_other(to),
        )

    def large_near_copy(d):
        to = (u + d) % HALF
        return remote(large_send.at[to], large_near.at[u], ln_s.at[to], ln_r.at[u], seq=in_half(to))

    def peer(d):
        return (me + d) % (HEADSETS * HALF)

    def att_copy(source, target, send, recv):
        def copy(d):
            p = peer(d)
            return remote(
                source.at[p % HALF], target.at[h, u], send.at[p], recv.at[me],
                seq=in_half(p % HALF), head=p // HALF,
            )

        return copy

    def piece(side, part, start, count):
        return wout.at[side, pl.ds(pl.multiple_of(part * W + start, 16), count), :]

    def wz_copy(d):
        to = (h + d) % HEADSETS
        ref = piece(core, h, x * 64 + y * 16, 16)
        return remote(ref, ref, wz_s.at[to], wz_r.at[h], head=to)

    def y_place(i):
        return (y + 1 + i // 3) % 4, (h + 1 + i % 3) % HEADSETS

    def wy_copy(i):
        to, part = y_place(i)
        ref = piece(core, part, x * 64 + y * 16, 16)
        return remote(
            ref, ref, wy_s.at[to * 4 + part], wy_r.at[y * 4 + part], seq=in_half(to * 2 + core)
        )

    def x_place(i):
        return (x + i // 3) % DPS, (h + 1 + i % 3) % HEADSETS

    def wx_copy(i):
        to, part = x_place(i)
        ref = piece(core, part, x * 64, 64)
        return remote(ref, ref, wx_s.at[to * 4 + part], wx_r.at[x * 4 + part], dp=to)

    def wc_copy(i):
        at, part = x_place(i)
        ref = piece(core, part, at * 64, 64)
        return remote(
            ref, ref, wc_s.at[at * 4 + part], wc_r.at[at * 4 + part], seq=in_half(u + 1 - 2 * core)
        )

    def x_arrival(i):
        return piece(core, x_place(i)[1], x_place(i)[0] * 64, 64), wx_r.at[x_place(i)[0] * 4 + x_place(i)[1]]

    def c_arrival(i):
        return (
            piece(1 - core, x_place(i)[1], x_place(i)[0] * 64, 64),
            wc_r.at[x_place(i)[0] * 4 + x_place(i)[1]],
        )

    groups = {
        "mod_a": (1, HEADSETS, mod_a_copy, lambda d: (mod_a.at[(h + d) % HEADSETS], ma_r.at[(h + d) % HEADSETS])),
        "mod_b": (1, HALF, mod_b_copy, lambda d: (mod_b.at[(u + d) % HALF], mb_r.at[(u + d) % HALF])),
        "cache": (1, 16, cache_copy, lambda d: (cache_recv.at[(seq + d) % 16], ca_r.at[(seq + d) % 16])),
        "small_near": (
            1, HALF, small_near_copy, lambda d: (small_near.at[(u + d) % HALF], sn_r.at[(u + d) % HALF]),
        ),
        "small_far": (
            0, HALF, small_far_copy, lambda d: (small_far.at[(u + d) % HALF], sf_r.at[(u + d) % HALF]),
        ),
        "large_near": (
            1, HALF, large_near_copy, lambda d: (large_near.at[(u + d) % HALF], ln_r.at[(u + d) % HALF]),
        ),
        "att_small": (
            1, HEADSETS * HALF, att_copy(att_small, small_recv, as_s, as_r),
            lambda d: (small_recv.at[peer(d) // HALF, peer(d) % HALF], as_r.at[peer(d)]),
        ),
        "att_large": (
            1, HEADSETS * HALF, att_copy(att_large, large_recv, al_s, al_r),
            lambda d: (large_recv.at[peer(d) // HALF, peer(d) % HALF], al_r.at[peer(d)]),
        ),
        "wz": (
            1, HEADSETS, wz_copy,
            lambda d: (piece(core, (h + d) % HEADSETS, x * 64 + y * 16, 16), wz_r.at[(h + d) % HEADSETS]),
        ),
        "wy": (
            0, 9, wy_copy,
            lambda i: (
                piece(core, y_place(i)[1], x * 64 + y_place(i)[0] * 16, 16),
                wy_r.at[y_place(i)[0] * 4 + y_place(i)[1]],
            ),
        ),
        "wx": (3, 12, wx_copy, x_arrival),
        "wc": (0, 12, wc_copy, c_arrival),
    }

    def over(low, high, action):
        def step(d, c):
            action(d)
            return c

        lax.fori_loop(low, high, step, 0)

    def landed(place):
        slot, sem = place
        remote(slot, slot, ma_s.at[0], sem, head=(h + 1) % HEADSETS).wait_recv()

    def start(name):
        low, high, copy, _ = groups[name]
        over(low, high, lambda d: copy(d).start())

    def arrive(name):
        low, high, _, arrival = groups[name]
        over(low, high, lambda d: landed(arrival(d)))

    def sent(name):
        low, high, copy, _ = groups[name]
        over(low, high, lambda d: copy(d).wait_send())

    partner = [
        remote(position.at[0], far_position, fp_s.at[0], fp_r.at[0], seq=in_other(u)),
        remote(feature_sum, far_features, fp_s.at[1], fp_r.at[1], seq=in_other(u)),
    ]

    loads[0].wait()
    owned = table.shape[1]
    rows8 = iota((IMG, owned), 0)
    wanted = jnp.zeros((IMG, owned), jnp.int32)
    for b in range(IMG):
        wanted = jnp.where(rows8 == b, labels[b] - h * owned, wanted)
    onehot = flags(wanted == iota((IMG, owned), 1))
    parts = [dot(onehot, table[t]) for t in range(3)] + [jnp.zeros((IMG, W), F32)]
    mod_a[h] = jnp.concatenate(parts, axis=0).astype(BF16)

    pl.semaphore_wait(barrier, HEADSETS * HALF - 1 + HALF + DPS - 1)
    start("mod_a")
    for copy in partner:
        copy.start()

    group = flags((iota((W, W), 0) >> 6) == (iota((W, W), 1) >> 6))

    def normalize(v):
        high, low = split(v * v)
        return v * lax.rsqrt(dot(high, group) + dot(low, group) + 1e-06)

    r, c = iota((W, W), 0), iota((W, W), 1)
    to_kind = flags(c == ((r >> 5) * 32 + (r & 15) * 2 + ((r >> 4) & 1)))
    moved = dot(to_kind, cache[...].reshape(W, W))
    moved = jnp.where(((r >> 4) & 1) == 0, normalize(moved), moved)
    cache_send[...] = moved.astype(BF16).reshape(IMG, 32, W)
    cache_recv[seq] = cache_send[u]

    loads[4].wait()
    loads[5].wait()
    start("wz")

    taps = []
    for n, row in enumerate((seq, (seq + HALF) % 16)):
        place = 26 * row - 3 + 3 * ((16 - row) // 16)
        lower = place // 32
        upper = lower + 1 - lower // (S13 - 1)
        taps.append((place % 32).astype(F32) * (1.0 / 32.0))
        for t, source in enumerate((ids[lower], ids[upper])):
            for j in range(S13):
                id_lanes[2 * n + t, j] = jnp.broadcast_to(source[:, j : j + 1], (IMG, 128))
    loads[1].wait()

    def look(c, total):
        start_at = pl.multiple_of(c * SPAN, SPAN)
        columns = []
        for q in range(SPAN // 128):
            entry = iota((IMG, 128), 1) + (c * SPAN + q * 128)
            hits = []
            for n in range(2):
                for j in range(S13):
                    hits.append(
                        jnp.where(id_lanes[2 * n, j] == entry, 1.0 - taps[n], 0.0)
                        + jnp.where(id_lanes[2 * n + 1, j] == entry, taps[n], 0.0)
                    )
            columns.append(jnp.concatenate(hits, axis=0).astype(BF16))
        both = jnp.concatenate(split(codebook[:, pl.ds(start_at, SPAN)]), axis=0)
        return total + dot_nt(jnp.concatenate(columns, axis=1), both)

    looked = lax.fori_loop(0, codebook.shape[1] // SPAN, look, jnp.zeros((2 * SMALL, 64), F32))
    looked = looked[:, 0:32] + looked[:, 32:64]

    arrive("mod_a")
    total = mod_a[0].astype(F32)
    for part in range(1, HEADSETS):
        total = total + mod_a[part].astype(F32)
    mod_b[u] = total.astype(BF16)
    start("mod_b")
    start("cache")

    loads[3].wait()
    first = 2 * LARGE
    for i in range(SMALL // 16):
        xhat[first + 16 * i : first + 16 * i + 16, :] = layer_norm(thirteen[16 * i : 16 * i + 16, :].astype(F32))
    xhat[ROWS - 16 : ROWS - 8, :] = layer_norm(thirteen[SMALL - 8 : SMALL, :].astype(F32))
    xhat[ROWS - 8 : ROWS, :] = jnp.zeros((8, D), F32)
    arrive("wz")
    start("wy")
    loads[2].wait()
    embed_high, embed_low = split(embed[...])
    embed_parts = jnp.concatenate([embed_high, embed_low, embed_high], axis=0)
    bias_row = bias[...].reshape(1, D)

    def embedded(first, source, rows, table_rows):
        features = []
        for s in range(S16):
            at = max(26 * s - 3, 0)
            low = at // 32
            up = min(low + 1, S13 - 1)
            frac = (at % 32) / 32.0
            features.append(
                source[:, s * 32 : (s + 1) * 32]
                + rows[low * IMG : (low + 1) * IMG] * (1.0 - frac)
                + rows[up * IMG : (up + 1) * IMG] * frac
            )
        high, low = split(jnp.concatenate(features, axis=0))
        xhat[first : first + LARGE, :] = dot(jnp.concatenate([high, high, low], axis=1), embed_parts)
        for i in range(S16 // 2):
            pair = table_rows[2 * i : 2 * i + 2, :].astype(F32)
            pair = jnp.concatenate([jnp.broadcast_to(pair[k : k + 1], (IMG, D)) for k in range(2)], axis=0)
            at = first + 16 * i
            row = xhat[at : at + 16, :] + bias_row + pair
            xhat[at : at + 16, :] = layer_norm(row.astype(BF16).astype(F32))

    embedded(0, feature_sum[:, 0, :], looked[0:SMALL], position[0])
    for copy in partner:
        copy.wait_recv()
    embedded(LARGE, far_features[:, 0, :], looked[SMALL : 2 * SMALL], far_position[...])

    arrive("mod_b")
    for c in range(HALF):
        chunk = mod_b[c].astype(F32)
        if c == HALF - 1:
            chunk = chunk[:, 128:]
        width = chunk.shape[1]
        mod[0, :, c * W : c * W + width] = chunk[0:8]
        mod[1, :, c * W : c * W + width] = 1.0 + chunk[8:16]
        mod[2, :, c * W : c * W + width] = chunk[16:24]

    def modulate(i):
        at = pl.multiple_of(i * 16, 16)
        rows = xhat[pl.ds(at, 16), :].reshape(2, IMG, D)
        rows = rows * mod[1][None] + mod[0][None]
        xmod[pl.ds(at, 16), :] = rows.reshape(16, D).astype(BF16)

    lane_head = iota((1, W), 1) >> 6
    scales = jnp.zeros((1, W), F32)
    for k in range(4):
        scales = jnp.where(lane_head == k, head_scale[k], scales)

    def project(first, count, t):
        out = dot(xmod[first : first + count, :], qkv[t])
        if t == 0:
            out = normalize(out) * scales
        elif t == 1:
            out = normalize(out)
        return out.astype(BF16)

    over(2 * LARGE // 16, ROWS // 16, modulate)
    loads[6].wait()
    r, c = iota((LARGE, PADDED), 0), iota((LARGE, PADDED), 1)
    to_image = flags(((r & 15) < S13) & (c == (r & 15) * IMG + (r >> 4)))
    for t in (1, 2, 0):
        moved = dot(to_image, project(2 * LARGE, PADDED, t)).astype(BF16)
        small_send[:, t * TOK : (t + 1) * TOK, :] = moved.reshape(IMG, TOK, W)
        if t == 2:
            start("small_far")
    start("small_near")
    small_near[u] = small_send[u]

    over(0, 2 * LARGE // 16, modulate)
    r, c = iota((LARGE, LARGE), 0), iota((LARGE, LARGE), 1)
    to_image = flags(c == (r & 15) * IMG + (r >> 4))
    slot = 0
    for t, first in ((0, 0), (1, 0), (2, 0), (1, LARGE), (2, LARGE)):
        moved = dot(to_image, project(first, LARGE, t)).astype(BF16)
        large_send[:, slot * TOK : (slot + 1) * TOK, :] = moved.reshape(IMG, TOK, W)
        slot += 1
    start("large_near")
    large_near[u] = large_send[u]

    arrive("wy")
    start("wx")
    over(0, 3, lambda i: wc_copy(i).start())

    lanes = iota((W, W), 1) >> 6
    key = iota((W, W), 0)

    def by_head(rows):
        return [
            jnp.where(lanes[0:LARGE] == k, rows, jnp.zeros_like(rows)) for k in range(4)
        ]

    def offer(index, values, valid):
        for k in range(4):
            row = (index * 4 + k) * W
            use = lanes == k
            if valid is not None:
                use = use & valid
            vext[row : row + W, 0:W] = jnp.where(use, values, jnp.zeros_like(values))
            vext[row : row + W, W : 2 * W] = flags(use)

    def weigh(index, queries, keys):
        for k in range(4):
            column = (index * 4 + k) * W
            weights[:, column : column + W] = jnp.exp(dot_nt(queries[k], keys)).astype(BF16)

    def attend(queries, keys, out):
        for index, block in enumerate(keys):
            weigh(index, queries, block)
        used = len(keys) * 4 * W
        sums = dot(weights[:, 0:used], vext[0:used, :])
        out[...] = (sums[:, 0:W] / sums[:, W : 2 * W]).astype(BF16).reshape(HALF, TOK, W)

    arrive("cache")
    cache_keys = cache_recv[:, 0:16, :].reshape(W, W)
    offer(0, cache_recv[:, 16:32, :].reshape(W, W), key < W - 1)
    arrive("small_near")
    arrive("small_far")
    small_keys = jnp.concatenate(
        [small_near[:, TOK : 2 * TOK, :].reshape(LARGE, W), small_far[:, 0:TOK, :].reshape(LARGE, W)], axis=0
    )
    small_values = jnp.concatenate(
        [small_near[:, 2 * TOK : 3 * TOK, :].reshape(LARGE, W), small_far[:, TOK : 2 * TOK, :].reshape(LARGE, W)],
        axis=0,
    )
    map_row = (key >> 4) + HALF * zh * jnp.where(key < LARGE, 1, -1)
    offer(1, small_values, ((key & 15) < S13) & (map_row < S13))
    attend(by_head(small_near[:, 0:TOK, :].reshape(LARGE, W)), [cache_keys, small_keys], att_small)
    start("att_small")
    small_recv[h, u] = att_small[u]

    arrive("large_near")
    large_keys = jnp.concatenate(
        [large_near[:, k * TOK : (k + 1) * TOK, :].reshape(LARGE, W) for k in (1, 3)], axis=0
    )
    large_values = jnp.concatenate(
        [large_near[:, k * TOK : (k + 1) * TOK, :].reshape(LARGE, W) for k in (2, 4)], axis=0
    )
    offer(2, large_values, None)
    attend(
        by_head(large_near[:, 0:TOK, :].reshape(LARGE, W)), [cache_keys, small_keys, large_keys], att_large
    )
    start("att_large")
    large_recv[h, u] = att_large[u]

    def pass_on(i):
        landed(x_arrival(i))
        wc_copy(i).start()

    over(3, 12, pass_on)

    def columns():
        for first in range(0, D, W):
            width = min(W, D - first)
            side = 0 if first < WIDE else 1
            inner = first - side * SECOND
            yield first, first + width, wout.at[side, :, inner : inner + width]

    r, c = iota((PADDED, LARGE), 0), iota((PADDED, LARGE), 1)
    to_row = flags(c == (r & 7) * TOK + (r >> 3))
    arrive("att_small")
    for k in range(HEADSETS):
        small_all[:, k * W : (k + 1) * W] = dot(to_row, small_recv[k].reshape(LARGE, W)).astype(BF16)
    arrive("wc")
    kept = seq < S13
    for low, high, block in columns():
        branch = dot(small_all[...], block[...])
        gate = mod[2, :, low:high]
        for j in range(S13):
            rows = gate * branch[j * IMG : (j + 1) * IMG]
            o13[j, :, low:high] = jnp.where(kept, rows, jnp.zeros_like(rows)).astype(BF16)
    arrive("att_large")
    for k in range(HEADSETS):
        large_all[:, k * W : (k + 1) * W] = large_recv[k].reshape(LARGE, W)
    for low, high, block in columns():
        branch = dot(large_all[...], block[...])
        gate = mod[2, :, low:high]
        for b in range(IMG):
            o16[b, :, low:high] = (gate[b : b + 1] * branch[b * S16 : (b + 1) * S16]).astype(BF16)

    for copy in partner:
        copy.wait_send()
    for name in groups:
        sent(name)


def body(
    map_thirteen, kv_cache, class_labels, class_table, sampled_ids, codebook, feature_sum,
    embed_weight, embed_bias, position_table, qkv_weight, out_weight, head_scale,
):
    owned = class_table.shape[0]
    vocabulary = codebook.shape[0]
    vmem = pl.BlockSpec(memory_space=pltpu.VMEM)
    smem = pl.BlockSpec(memory_space=pltpu.SMEM)
    anywhere = pl.BlockSpec(memory_space=pl.ANY)
    dma = pltpu.SemaphoreType.DMA
    o13, o16 = pl.pallas_call(
        kernel,
        out_shape=(
            jax.ShapeDtypeStruct((S13, IMG, D), BF16),
            jax.ShapeDtypeStruct((IMG, S16, D), BF16),
        ),
        in_specs=[smem, smem, vmem, vmem, vmem, vmem, vmem] + [anywhere] * 6,
        out_specs=(vmem, vmem),
        scratch_shapes=[
            pltpu.VMEM((SMALL, D), BF16),
            pltpu.VMEM((3, owned, W), BF16),
            pltpu.VMEM((32, vocabulary), F32),
            pltpu.VMEM((32, D), F32),
            pltpu.VMEM((3, D, W), BF16),
            pltpu.VMEM((2, HEADSETS * W, WIDE), BF16),
            pltpu.VMEM((IMG, 32, W), BF16),
            pltpu.VMEM((16, 32, W), BF16),
            pltpu.VMEM((HEADSETS, 32, W), BF16),
            pltpu.VMEM((HALF, 32, W), BF16),
            pltpu.VMEM((3, IMG, D), F32),
            pltpu.VMEM((S16, D), BF16),
            pltpu.VMEM((IMG, 1, S16 * 32), F32),
            pltpu.VMEM((4, S13, IMG, 128), jnp.int32),
            pltpu.VMEM((ROWS, D), F32),
            pltpu.VMEM((ROWS, D), BF16),
            pltpu.VMEM((IMG, 3 * TOK, W), BF16),
            pltpu.VMEM((HALF, 3 * TOK, W), BF16),
            pltpu.VMEM((HALF, 2 * TOK, W), BF16),
            pltpu.VMEM((IMG, 5 * TOK, W), BF16),
            pltpu.VMEM((HALF, 5 * TOK, W), BF16),
            pltpu.VMEM((LARGE, 12 * W), BF16),
            pltpu.VMEM((12 * W, 2 * W), BF16),
            pltpu.VMEM((HALF, TOK, W), BF16),
            pltpu.VMEM((HALF, TOK, W), BF16),
            pltpu.VMEM((HEADSETS, HALF, TOK, W), BF16),
            pltpu.VMEM((HEADSETS, HALF, TOK, W), BF16),
            pltpu.VMEM((PADDED, HEADSETS * W), BF16),
            pltpu.VMEM((LARGE, HEADSETS * W), BF16),
            dma((8,)),
        ]
        + [dma((n,)) for n in (4, 4, 8, 8, 2, 2, 16, 16, 8, 8, 8, 8, 8, 8, 32, 32, 32, 32, 4, 4, 16, 16, 16, 16, 16, 16)],
        compiler_params=pltpu.CompilerParams(
            collective_id=0, has_side_effects=True, vmem_limit_bytes=VMEM_LIMIT
        ),
        cost_estimate=pl.CostEstimate(flops=3_000_000_000, bytes_accessed=12_000_000, transcendentals=1_000_000),
    )(
        class_labels,
        head_scale,
        sampled_ids.transpose(1, 0, 2),
        kv_cache,
        feature_sum,
        embed_bias,
        position_table,
        map_thirteen.reshape(IMG, S13, D).transpose(1, 0, 2).reshape(SMALL, D),
        class_table.transpose(1, 0, 2),
        codebook.T,
        embed_weight,
        qkv_weight.transpose(1, 0, 2),
        out_weight,
    )
    return o13.transpose(1, 0, 2)[:, None], o16[:, None]


def solution(mesh):
    placed = (
        P("dp", "seq", None, None),
        P("dp", "seq", None, "head"),
        P("dp"),
        P("head", None, None),
        P("dp", None, None),
        P(),
        P("dp", "seq", None),
        P(),
        P(),
        P("seq", None, None),
        P(None, None, "head"),
        P("head", None),
        P("head"),
    )
    return jax.shard_map(
        body,
        mesh=mesh,
        in_specs=placed,
        out_specs=(P("dp", "seq", None, None), P("dp", "seq", None, None)),
        check_vma=False,
    )
```

time: 67.6 us -> 71.1 us (1.052)
  the two profiles are of different devices: /device:TPU:255 before, /device:TPU:1 now
where the time goes in v2:
time: 71.1 us; the launch traced here: 70.9 us
  Pallas kernels  66.7 us (94%)
  local copies, waits for them, and re-layouts  3.62 us (5%)
    pallas_call x1, Pallas kernels, body(): pl.pallas_call(kernel, out_shape=(jax.ShapeDtypeStruct((S13, IMG, D), BF1...  66.7 us
    unnamed x2, local copies, waits for them, and re-layouts  3.62 us

profile of v2, /device:TPU:1, one launch (start us, length us, event | category | flops | bytes accessed | tf_op | source)
XLA Modules:
  0.0 70.9 jit_solution(7370847515079753868)
XLA Ops:
  0.6 66.7 %shard_map.140 = (bf16[13,8,1920]{2,1,0:T(8,128)(2,1)}, bf16[8,16,1920]{2,1,0:T(8,128)(2,1)}) custom-call(s32[8]{0:T(128)} %labels.1, f32[4]{0:T(128)} %head_scale.1, s32[13,8,13]{2,1,0:T(8,128)} %bitcast.21, bf16[8,16,2,256]{3,2,1,0:T(2,128)(2,1)} %cache.1, f32[8,1,512]{2,1,0:T(1,128)} %feature_sum.1, f32[1920]{0:T(1024)} %bias.1, ...), custom_call_target="tpu_custom_call" | custom-call | flops 3000000000 | bytes 12000000 | tf_op jit(solution)/shard_map/pallas_call | solution.py:550
  67.3 1.8 %copy.18 = bf16[8,1,13,1920]{3,0,2,1:T(8,128)(2,1)} copy(bf16[8,1,13,1920]{3,0,2,1:T(8,128)(2,1)} %bitcast.16) | data formatting | bytes 798720
  69.1 1.8 %copy.19 = bf16[8,1,16,1920]{3,2,1,0:T(8,128)(2,1)} copy(bf16[8,1,16,1920]{3,2,1,0:T(8,128)(2,1)} %bitcast.15) | data formatting | bytes 983040

commit v3 on v2

--- a/solution.py
+++ b/solution.py
@@ -22,6 +22,7 @@
 PADDED = SMALL + IMG
 ROWS = 2 * LARGE + PADDED
 SPAN = 512
+VIA_X = 768
 WIDE = 1024
 SECOND = D - WIDE
 F32 = jnp.float32
@@ -63,16 +64,18 @@
 
 
 def kernel(
-    labels, head_scale, ids, cache, feature_sum, bias, position,
+    labels_hbm, scale_hbm, ids_hbm, cache_hbm, features_hbm, bias_hbm, position_hbm,
     thirteen_hbm, table_hbm, codebook_hbm, embed_hbm, qkv_hbm, out_hbm,
     o13, o16,
+    labels, head_scale, ids, cache, feature_sum, bias, position,
     thirteen, table, codebook, embed, qkv, wout,
     cache_send, cache_recv, mod_a, mod_b, mod, far_position, far_features, id_lanes, xhat, xmod,
     small_send, small_near, small_far, large_send, large_near,
     weights, vext, att_small, att_large, small_recv, large_recv, small_all, large_all,
     local_sem,
     ma_s, ma_r, mb_s, mb_r, fp_s, fp_r, ca_s, ca_r, sn_s, sn_r, sf_s, sf_r, ln_s, ln_r,
-    as_s, as_r, al_s, al_r, wz_s, wz_r, wy_s, wy_r, wx_s, wx_r, wc_s, wc_r,
+    as_s, as_r, al_s, al_r, fs_s, fl_s,
+    wz_s, wz_r, ay_s, ay_r, bx_s, bx_r, ax_s, ax_r, by_s, by_r, wc_s, wc_r,
 ):
     x = lax.axis_index("dp")
     seq = lax.axis_index("seq")
@@ -87,20 +90,6 @@
     def in_other(place):
         return (1 - zh) * HALF + place
 
-    col0 = pl.multiple_of(u * W - (u // 7) * 128, 128)
-    loads = [
-        (table_hbm.at[:, :, pl.ds(col0, W)], table),
-        (codebook_hbm, codebook),
-        (embed_hbm, embed),
-        (thirteen_hbm, thirteen),
-        (out_hbm.at[:, pl.ds(0, WIDE)], wout.at[0, pl.ds(pl.multiple_of(h * W, W), W), :]),
-        (out_hbm.at[:, pl.ds(SECOND, WIDE)], wout.at[1, pl.ds(pl.multiple_of(h * W, W), W), :]),
-        (qkv_hbm, qkv),
-    ]
-    loads = [pltpu.make_async_copy(a, b, local_sem.at[i]) for i, (a, b) in enumerate(loads)]
-    for load in loads:
-        load.start()
-
     barrier = pltpu.get_barrier_semaphore()
 
     def greet_half(d, c):
@@ -120,9 +109,36 @@
         pl.semaphore_signal(barrier, inc=1, device_id={"dp": (x + d) % DPS}, device_id_type=MESH)
         return c
 
+    lax.fori_loop(0, HALF, greet_other, 0)
     lax.fori_loop(1, HEADSETS * HALF, greet_half, 0)
-    lax.fori_loop(0, HALF, greet_other, 0)
     lax.fori_loop(1, DPS, greet_dp, 0)
+
+    col0 = pl.multiple_of(u * W - (u // 7) * 128, 128)
+    loads = [
+        (labels_hbm, labels),
+        (table_hbm.at[:, :, pl.ds(col0, W)], table),
+        (cache_hbm, cache),
+        (position_hbm, position),
+        (features_hbm, feature_sum),
+        (ids_hbm, ids),
+        (codebook_hbm, codebook),
+        (out_hbm.at[:, pl.ds(0, WIDE)], wout.at[0, pl.ds(pl.multiple_of(h * W, W), W), :]),
+        (out_hbm.at[:, pl.ds(SECOND, WIDE)], wout.at[1, pl.ds(pl.multiple_of(h * W, W), W), :]),
+        (thirteen_hbm, thirteen),
+        (embed_hbm, embed),
+        (bias_hbm, bias),
+        (scale_hbm, head_scale),
+        (qkv_hbm, qkv),
+    ]
+    names = (
+        "labels", "table", "cache", "position", "features", "ids", "codebook", "out0", "out1", "thirteen",
+        "embed", "bias", "scale", "qkv",
+    )
+    loads = {
+        name: pltpu.make_async_copy(a, b, local_sem.at[i]) for i, (name, (a, b)) in enumerate(zip(names, loads))
+    }
+    for load in loads.values():
+        load.start()
 
     def mod_a_copy(d):
         to = (h + d) % HEADSETS
@@ -154,57 +170,115 @@
     def peer(d):
         return (me + d) % (HEADSETS * HALF)
 
-    def att_copy(source, target, send, recv):
-        def copy(d):
-            p = peer(d)
+    relay = (h % 3) > 0
+    relayed, beyond = 3 * (2 - h), 3 * (h - 1)
+
+    class Gather:
+        def __init__(self, source, target, send, recv, forward):
+            self.source, self.target, self.send, self.recv, self.forward = source, target, send, recv, forward
+
+        def copy(self, p):
             return remote(
-                source.at[p % HALF], target.at[h, u], send.at[p], recv.at[me],
+                self.source.at[p % HALF], self.target.at[h, u], self.send.at[p], self.recv.at[me],
                 seq=in_half(p % HALF), head=p // HALF,
             )
 
-        return copy
-
-    def piece(side, part, start, count):
-        return wout.at[side, pl.ds(pl.multiple_of(part * W + start, 16), count), :]
-
-    def wz_copy(d):
-        to = (h + d) % HEADSETS
-        ref = piece(core, h, x * 64 + y * 16, 16)
+        def direct(self, action):
+            def step(d):
+                p = peer(d)
+
+                getattr(self.copy(p), action)()
+
+            over(1, HEADSETS * HALF, step)
+
+        def start(self):
+            self.direct("start")
+            self.target[h, u] = self.source[u]
+
+        def slot(self, part, b):
+            return self.target.at[part, b], self.recv.at[part * HALF + b]
+
+        def passing(self, b):
+            ref, sem = self.slot(relayed, b)
+            return remote(ref, ref, self.forward.at[b], sem, head=beyond)
+
+        def pass_on(self):
+            @pl.when(relay)
+            def _():
+                def step(d):
+                    b = (u + d) % HALF
+                    landed(self.slot(relayed, b))
+                    self.passing(b).start()
+
+                over(0, HALF, step)
+
+        def arrive(self):
+            def step(d):
+                p = peer(d)
+
+                landed(self.slot(p // HALF, p % HALF))
+
+            over(1, HEADSETS * HALF, step)
+
+        def sent(self):
+            self.direct("wait_send")
+
+    gathers = [
+        Gather(att_small, small_recv, as_s, as_r, fs_s),
+        Gather(att_large, large_recv, al_s, al_r, fl_s),
+    ]
+
+    def piece(part, column, start, count):
+        rows = pl.ds(pl.multiple_of(part * W + start, 16), count)
+        return wout.at[core, rows, 0:VIA_X] if column == 0 else wout.at[core, rows, VIA_X:WIDE]
+
+    def first_rows(column):
+        return x * 64 + y * 16 if column == 0 else y * 64 + x * 16
+
+    def wz_copy(i):
+        to = (h + 1 + i) % HEADSETS
+        ref = piece(h, 0, first_rows(0), 16)
         return remote(ref, ref, wz_s.at[to], wz_r.at[h], head=to)
+
+    def vz_copy(i):
+        to = (h + 1 + i) % HEADSETS
+        ref = piece(h, 1, first_rows(1), 16)
+        return remote(ref, ref, wz_s.at[4 + to], wz_r.at[4 + h], head=to)
 
     def y_place(i):
         return (y + 1 + i // 3) % 4, (h + 1 + i % 3) % HEADSETS
 
-    def wy_copy(i):
+    def x_place(i):
+        return (x + 1 + i // 3) % DPS, (h + 1 + i % 3) % HEADSETS
+
+    def ay_copy(i):
         to, part = y_place(i)
-        ref = piece(core, part, x * 64 + y * 16, 16)
+        ref = piece(part, 0, first_rows(0), 16)
         return remote(
-            ref, ref, wy_s.at[to * 4 + part], wy_r.at[y * 4 + part], seq=in_half(to * 2 + core)
+            ref, ref, ay_s.at[to * 4 + part], ay_r.at[y * 4 + part], seq=in_half(to * 2 + core)
         )
 
-    def x_place(i):
-        return (x + i // 3) % DPS, (h + 1 + i % 3) % HEADSETS
-
-    def wx_copy(i):
+    def bx_copy(i):
         to, part = x_place(i)
-        ref = piece(core, part, x * 64, 64)
-        return remote(ref, ref, wx_s.at[to * 4 + part], wx_r.at[x * 4 + part], dp=to)
+        ref = piece(part, 1, first_rows(1), 16)
+        return remote(ref, ref, bx_s.at[to * 4 + part], bx_r.at[x * 4 + part], dp=to)
+
+    def ax_copy(i):
+        to, part = x_place(i)
+        ref = piece(part, 0, x * 64, 64)
+        return remote(ref, ref, ax_s.at[to * 4 + part], ax_r.at[x * 4 + part], dp=to)
+
+    def by_copy(i):
+        to, part = y_place(i)
+        ref = piece(part, 1, y * 64, 64)
+        return remote(
+            ref, ref, by_s.at[to * 4 + part], by_r.at[y * 4 + part], seq=in_half(to * 2 + core)
+        )
 
     def wc_copy(i):
-        at, part = x_place(i)
-        ref = piece(core, part, at * 64, 64)
-        return remote(
-            ref, ref, wc_s.at[at * 4 + part], wc_r.at[at * 4 + part], seq=in_half(u + 1 - 2 * core)
-        )
-
-    def x_arrival(i):
-        return piece(core, x_place(i)[1], x_place(i)[0] * 64, 64), wx_r.at[x_place(i)[0] * 4 + x_place(i)[1]]
-
-    def c_arrival(i):
-        return (
-            piece(1 - core, x_place(i)[1], x_place(i)[0] * 64, 64),
-            wc_r.at[x_place(i)[0] * 4 + x_place(i)[1]],
-        )
+        part = (h + 1 + i) % HEADSETS
+        ref = wout.at[core, pl.ds(pl.multiple_of(part * W, W), W), :]
+        return remote(ref, ref, wc_s.at[part], wc_r.at[part], seq=in_half(u + 1 - 2 * core))
 
     groups = {
         "mod_a": (1, HEADSETS, mod_a_copy, lambda d: (mod_a.at[(h + d) % HEADSETS], ma_r.at[(h + d) % HEADSETS])),
@@ -219,27 +293,47 @@
         "large_near": (
             1, HALF, large_near_copy, lambda d: (large_near.at[(u + d) % HALF], ln_r.at[(u + d) % HALF]),
         ),
-        "att_small": (
-            1, HEADSETS * HALF, att_copy(att_small, small_recv, as_s, as_r),
-            lambda d: (small_recv.at[peer(d) // HALF, peer(d) % HALF], as_r.at[peer(d)]),
-        ),
-        "att_large": (
-            1, HEADSETS * HALF, att_copy(att_large, large_recv, al_s, al_r),
-            lambda d: (large_recv.at[peer(d) // HALF, peer(d) % HALF], al_r.at[peer(d)]),
-        ),
         "wz": (
-            1, HEADSETS, wz_copy,
-            lambda d: (piece(core, (h + d) % HEADSETS, x * 64 + y * 16, 16), wz_r.at[(h + d) % HEADSETS]),
-        ),
-        "wy": (
-            0, 9, wy_copy,
+            0, 3, wz_copy,
+            lambda i: (piece((h + 1 + i) % HEADSETS, 0, first_rows(0), 16), wz_r.at[(h + 1 + i) % HEADSETS]),
+        ),
+        "vz": (
+            0, 3, vz_copy,
+            lambda i: (piece((h + 1 + i) % HEADSETS, 1, first_rows(1), 16), wz_r.at[4 + (h + 1 + i) % HEADSETS]),
+        ),
+        "ay": (
+            0, 9, ay_copy,
             lambda i: (
-                piece(core, y_place(i)[1], x * 64 + y_place(i)[0] * 16, 16),
-                wy_r.at[y_place(i)[0] * 4 + y_place(i)[1]],
+                piece(y_place(i)[1], 0, x * 64 + y_place(i)[0] * 16, 16),
+                ay_r.at[y_place(i)[0] * 4 + y_place(i)[1]],
             ),
         ),
-        "wx": (3, 12, wx_copy, x_arrival),
-        "wc": (0, 12, wc_copy, c_arrival),
+        "bx": (
+            0, 9, bx_copy,
+            lambda i: (
+                piece(x_place(i)[1], 1, y * 64 + x_place(i)[0] * 16, 16),
+                bx_r.at[x_place(i)[0] * 4 + x_place(i)[1]],
+            ),
+        ),
+        "ax": (
+            0, 9, ax_copy,
+            lambda i: (
+                piece(x_place(i)[1], 0, x_place(i)[0] * 64, 64), ax_r.at[x_place(i)[0] * 4 + x_place(i)[1]],
+            ),
+        ),
+        "by": (
+            0, 9, by_copy,
+            lambda i: (
+                piece(y_place(i)[1], 1, y_place(i)[0] * 64, 64), by_r.at[y_place(i)[0] * 4 + y_place(i)[1]],
+            ),
+        ),
+        "wc": (
+            0, 3, wc_copy,
+            lambda i: (
+                wout.at[1 - core, pl.ds(pl.multiple_of(((h + 1 + i) % HEADSETS) * W, W), W), :],
+                wc_r.at[(h + 1 + i) % HEADSETS],
+            ),
+        ),
     }
 
     def over(low, high, action):
@@ -270,7 +364,8 @@
         remote(feature_sum, far_features, fp_s.at[1], fp_r.at[1], seq=in_other(u)),
     ]
 
-    loads[0].wait()
+    loads["labels"].wait()
+    loads["table"].wait()
     owned = table.shape[1]
     rows8 = iota((IMG, owned), 0)
     wanted = jnp.zeros((IMG, owned), jnp.int32)
@@ -280,27 +375,31 @@
     parts = [dot(onehot, table[t]) for t in range(3)] + [jnp.zeros((IMG, W), F32)]
     mod_a[h] = jnp.concatenate(parts, axis=0).astype(BF16)
 
-    pl.semaphore_wait(barrier, HEADSETS * HALF - 1 + HALF + DPS - 1)
-    start("mod_a")
-    for copy in partner:
-        copy.start()
-
     group = flags((iota((W, W), 0) >> 6) == (iota((W, W), 1) >> 6))
 
     def normalize(v):
         high, low = split(v * v)
         return v * lax.rsqrt(dot(high, group) + dot(low, group) + 1e-06)
 
+    loads["cache"].wait()
     r, c = iota((W, W), 0), iota((W, W), 1)
     to_kind = flags(c == ((r >> 5) * 32 + (r & 15) * 2 + ((r >> 4) & 1)))
     moved = dot(to_kind, cache[...].reshape(W, W))
     moved = jnp.where(((r >> 4) & 1) == 0, normalize(moved), moved)
     cache_send[...] = moved.astype(BF16).reshape(IMG, 32, W)
     cache_recv[seq] = cache_send[u]
-
-    loads[4].wait()
-    loads[5].wait()
+    loads["position"].wait()
+    loads["features"].wait()
+    loads["ids"].wait()
+
+    pl.semaphore_wait(barrier, HEADSETS * HALF - 1 + HALF + DPS - 1)
+    start("mod_a")
+    for copy in partner:
+        copy.start()
+    loads["out0"].wait()
+    loads["out1"].wait()
     start("wz")
+    start("vz")
 
     taps = []
     for n, row in enumerate((seq, (seq + HALF) % 16)):
@@ -311,7 +410,7 @@
         for t, source in enumerate((ids[lower], ids[upper])):
             for j in range(S13):
                 id_lanes[2 * n + t, j] = jnp.broadcast_to(source[:, j : j + 1], (IMG, 128))
-    loads[1].wait()
+    loads["codebook"].wait()
 
     def look(c, total):
         start_at = pl.multiple_of(c * SPAN, SPAN)
@@ -340,15 +439,14 @@
     start("mod_b")
     start("cache")
 
-    loads[3].wait()
+    loads["thirteen"].wait()
     first = 2 * LARGE
     for i in range(SMALL // 16):
         xhat[first + 16 * i : first + 16 * i + 16, :] = layer_norm(thirteen[16 * i : 16 * i + 16, :].astype(F32))
     xhat[ROWS - 16 : ROWS - 8, :] = layer_norm(thirteen[SMALL - 8 : SMALL, :].astype(F32))
     xhat[ROWS - 8 : ROWS, :] = jnp.zeros((8, D), F32)
-    arrive("wz")
-    start("wy")
-    loads[2].wait()
+    loads["embed"].wait()
+    loads["bias"].wait()
     embed_high, embed_low = split(embed[...])
     embed_parts = jnp.concatenate([embed_high, embed_low, embed_high], axis=0)
     bias_row = bias[...].reshape(1, D)
@@ -379,6 +477,10 @@
         copy.wait_recv()
     embedded(LARGE, far_features[:, 0, :], looked[SMALL : 2 * SMALL], far_position[...])
 
+    arrive("wz")
+    arrive("vz")
+    start("ay")
+    start("bx")
     arrive("mod_b")
     for c in range(HALF):
         chunk = mod_b[c].astype(F32)
@@ -395,45 +497,44 @@
         rows = rows * mod[1][None] + mod[0][None]
         xmod[pl.ds(at, 16), :] = rows.reshape(16, D).astype(BF16)
 
+    loads["scale"].wait()
     lane_head = iota((1, W), 1) >> 6
     scales = jnp.zeros((1, W), F32)
     for k in range(4):
         scales = jnp.where(lane_head == k, head_scale[k], scales)
 
-    def project(first, count, t):
-        out = dot(xmod[first : first + count, :], qkv[t])
-        if t == 0:
-            out = normalize(out) * scales
-        elif t == 1:
-            out = normalize(out)
-        return out.astype(BF16)
-
-    over(2 * LARGE // 16, ROWS // 16, modulate)
-    loads[6].wait()
+    over(0, ROWS // 16, modulate)
+    loads["qkv"].wait()
     r, c = iota((LARGE, PADDED), 0), iota((LARGE, PADDED), 1)
-    to_image = flags(((r & 15) < S13) & (c == (r & 15) * IMG + (r >> 4)))
-    for t in (1, 2, 0):
-        moved = dot(to_image, project(2 * LARGE, PADDED, t)).astype(BF16)
-        small_send[:, t * TOK : (t + 1) * TOK, :] = moved.reshape(IMG, TOK, W)
-        if t == 2:
-            start("small_far")
+    small_to_image = flags(((r & 15) < S13) & (c == (r & 15) * IMG + (r >> 4)))
+    r, c = iota((LARGE, LARGE), 0), iota((LARGE, LARGE), 1)
+    large_to_image = flags(c == (r & 15) * IMG + (r >> 4))
+
+    def moved_small(rows):
+        return dot(small_to_image, rows).astype(BF16).reshape(IMG, TOK, W)
+
+    def moved_large(rows):
+        return dot(large_to_image, rows).astype(BF16).reshape(IMG, TOK, W)
+
+    keys = normalize(dot(xmod[...], qkv[1])).astype(BF16)
+    small_send[:, TOK : 2 * TOK, :] = moved_small(keys[2 * LARGE :])
+    values = dot(xmod[...], qkv[2]).astype(BF16)
+    small_send[:, 2 * TOK : 3 * TOK, :] = moved_small(values[2 * LARGE :])
+    start("small_far")
+    for slot, rows in ((1, keys[0:LARGE]), (2, values[0:LARGE]), (3, keys[LARGE : 2 * LARGE]), (4, values[LARGE : 2 * LARGE])):
+        large_send[:, slot * TOK : (slot + 1) * TOK, :] = moved_large(rows)
+    small_queries = normalize(dot(xmod[2 * LARGE :, :], qkv[0])) * scales
+    small_send[:, 0:TOK, :] = moved_small(small_queries.astype(BF16))
     start("small_near")
     small_near[u] = small_send[u]
-
-    over(0, 2 * LARGE // 16, modulate)
-    r, c = iota((LARGE, LARGE), 0), iota((LARGE, LARGE), 1)
-    to_image = flags(c == (r & 15) * IMG + (r >> 4))
-    slot = 0
-    for t, first in ((0, 0), (1, 0), (2, 0), (1, LARGE), (2, LARGE)):
-        moved = dot(to_image, project(first, LARGE, t)).astype(BF16)
-        large_send[:, slot * TOK : (slot + 1) * TOK, :] = moved.reshape(IMG, TOK, W)
-        slot += 1
+    large_queries = normalize(dot(xmod[0:LARGE, :], qkv[0])) * scales
+    large_send[:, 0:TOK, :] = moved_large(large_queries.astype(BF16))
     start("large_near")
     large_near[u] = large_send[u]
-
-    arrive("wy")
-    start("wx")
-    over(0, 3, lambda i: wc_copy(i).start())
+    arrive("ay")
+    arrive("bx")
+    start("ax")
+    start("by")
 
     lanes = iota((W, W), 1) >> 6
     key = iota((W, W), 0)
@@ -479,8 +580,7 @@
     map_row = (key >> 4) + HALF * zh * jnp.where(key < LARGE, 1, -1)
     offer(1, small_values, ((key & 15) < S13) & (map_row < S13))
     attend(by_head(small_near[:, 0:TOK, :].reshape(LARGE, W)), [cache_keys, small_keys], att_small)
-    start("att_small")
-    small_recv[h, u] = att_small[u]
+    gathers[0].start()
 
     arrive("large_near")
     large_keys = jnp.concatenate(
@@ -493,48 +593,69 @@
     attend(
         by_head(large_near[:, 0:TOK, :].reshape(LARGE, W)), [cache_keys, small_keys, large_keys], att_large
     )
-    start("att_large")
-    large_recv[h, u] = att_large[u]
-
-    def pass_on(i):
-        landed(x_arrival(i))
-        wc_copy(i).start()
-
-    over(3, 12, pass_on)
-
-    def columns():
-        for first in range(0, D, W):
-            width = min(W, D - first)
-            side = 0 if first < WIDE else 1
-            inner = first - side * SECOND
-            yield first, first + width, wout.at[side, :, inner : inner + width]
+    gathers[1].start()
+    arrive("ax")
+    arrive("by")
+    start("wc")
 
     r, c = iota((PADDED, LARGE), 0), iota((PADDED, LARGE), 1)
     to_row = flags(c == (r & 7) * TOK + (r >> 3))
-    arrive("att_small")
+    kept = seq < S13
+
+    def project_small(side):
+        def step(i):
+            inner = pl.multiple_of(i * W, W)
+            outer = pl.ds(pl.multiple_of(side * SECOND + inner, 128), W)
+            branch = dot(small_all[...], wout[side, :, pl.ds(inner, W)])
+            gate = mod[2, :, outer]
+            for j in range(S13):
+                rows = gate * branch[j * IMG : (j + 1) * IMG]
+                o13[j, :, outer] = jnp.where(kept, rows, jnp.zeros_like(rows)).astype(BF16)
+
+        over(0, WIDE // W, step)
+
+    def project_large(side):
+        def step(i):
+            inner = pl.multiple_of(i * W, W)
+            outer = pl.ds(pl.multiple_of(side * SECOND + inner, 128), W)
+            branch = dot(large_all[...], wout[side, :, pl.ds(inner, W)])
+            gate = mod[2, :, outer]
+            for b in range(IMG):
+                o16[b, :, outer] = (gate[b : b + 1] * branch[b * S16 : (b + 1) * S16]).astype(BF16)
+
+        over(0, WIDE // W, step)
+
+    gathers[0].arrive()
     for k in range(HEADSETS):
         small_all[:, k * W : (k + 1) * W] = dot(to_row, small_recv[k].reshape(LARGE, W)).astype(BF16)
-    arrive("wc")
-    kept = seq < S13
-    for low, high, block in columns():
-        branch = dot(small_all[...], block[...])
-        gate = mod[2, :, low:high]
-        for j in range(S13):
-            rows = gate * branch[j * IMG : (j + 1) * IMG]
-            o13[j, :, low:high] = jnp.where(kept, rows, jnp.zeros_like(rows)).astype(BF16)
-    arrive("att_large")
+    project_small(core)
+    gathers[1].arrive()
     for k in range(HEADSETS):
         large_all[:, k * W : (k + 1) * W] = large_recv[k].reshape(LARGE, W)
-    for low, high, block in columns():
-        branch = dot(large_all[...], block[...])
-        gate = mod[2, :, low:high]
-        for b in range(IMG):
-            o16[b, :, low:high] = (gate[b : b + 1] * branch[b * S16 : (b + 1) * S16]).astype(BF16)
+    project_large(core)
+    arrive("wc")
+    project_small(1 - core)
+    project_large(1 - core)
 
     for copy in partner:
         copy.wait_send()
     for name in groups:
         sent(name)
+    for gather in gathers:
+        gather.sent()
+
+
+def hand_on(a_ref, b_ref, a_out, b_out, sem):
+    copies = [
+        pltpu.make_async_copy(source.at[i : i + n], target.at[i : i + n], sem.at[k])
+        for k, (source, target, i, n) in enumerate(
+            ((a_ref, a_out, 0, 7), (a_ref, a_out, 7, 6), (b_ref, b_out, 0, 4), (b_ref, b_out, 4, 4))
+        )
+    ]
+    for copy in copies:
+        copy.start()
+    for copy in copies:
+        copy.wait()
 
 
 def body(
@@ -544,7 +665,6 @@
     owned = class_table.shape[0]
     vocabulary = codebook.shape[0]
     vmem = pl.BlockSpec(memory_space=pltpu.VMEM)
-    smem = pl.BlockSpec(memory_space=pltpu.SMEM)
     anywhere = pl.BlockSpec(memory_space=pl.ANY)
     dma = pltpu.SemaphoreType.DMA
     o13, o16 = pl.pallas_call(
@@ -553,9 +673,16 @@
             jax.ShapeDtypeStruct((S13, IMG, D), BF16),
             jax.ShapeDtypeStruct((IMG, S16, D), BF16),
         ),
-        in_specs=[smem, smem, vmem, vmem, vmem, vmem, vmem] + [anywhere] * 6,
+        in_specs=[anywhere] * 13,
         out_specs=(vmem, vmem),
         scratch_shapes=[
+            pltpu.SMEM((IMG,), jnp.int32),
+            pltpu.SMEM(head_scale.shape, F32),
+            pltpu.VMEM((S13, IMG, S13), jnp.int32),
+            pltpu.VMEM((IMG, 16, 2, W), BF16),
+            pltpu.VMEM((IMG, 1, S16 * 32), F32),
+            pltpu.VMEM((D,), F32),
+            pltpu.VMEM((1, S16, D), BF16),
             pltpu.VMEM((SMALL, D), BF16),
             pltpu.VMEM((3, owned, W), BF16),
             pltpu.VMEM((32, vocabulary), F32),
@@ -585,9 +712,11 @@
             pltpu.VMEM((HEADSETS, HALF, TOK, W), BF16),
             pltpu.VMEM((PADDED, HEADSETS * W), BF16),
             pltpu.VMEM((LARGE, HEADSETS * W), BF16),
-            dma((8,)),
+            dma((14,)),
         ]
-        + [dma((n,)) for n in (4, 4, 8, 8, 2, 2, 16, 16, 8, 8, 8, 8, 8, 8, 32, 32, 32, 32, 4, 4, 16, 16, 16, 16, 16, 16)],
+        + [dma((n,)) for n in (
+            4, 4, 8, 8, 2, 2, 16, 16, 8, 8, 8, 8, 8, 8, 32, 32, 32, 32, 8, 8, 8, 8, 16, 16, 16, 16, 16, 16, 16, 16, 4, 4
+        )],
         compiler_params=pltpu.CompilerParams(
             collective_id=0, has_side_effects=True, vmem_limit_bytes=VMEM_LIMIT
         ),
@@ -607,6 +736,17 @@
         qkv_weight.transpose(1, 0, 2),
         out_weight,
     )
+    o13, o16 = pl.pallas_call(
+        hand_on,
+        out_shape=(
+            jax.ShapeDtypeStruct((S13, IMG, D), BF16),
+            jax.ShapeDtypeStruct((IMG, S16, D), BF16),
+        ),
+        in_specs=[vmem] * 2,
+        out_specs=(anywhere, anywhere),
+        scratch_shapes=[dma((4,))],
+        cost_estimate=pl.CostEstimate(flops=0, bytes_accessed=1_800_000, transcendentals=0),
+    )(o13, o16)
     return o13.transpose(1, 0, 2)[:, None], o16[:, None]
 
 

time: 71.1 us -> 63.9 us (0.90)
  local copies, waits for them, and re-layouts: 3.62 us -> 0 us
  Pallas kernels: 66.7 us -> 63.1 us
    pallas_call x1, Pallas kernels: 66.7 us -> 61 us  [body(): pl.pallas_call(kernel, out_shape=(jax.ShapeDtypeStruct((S13, IMG, D), BF1...]
    unnamed x2 -> x0, local copies, waits for them, and re-layouts: 3.62 us -> none
    pallas_call x0 -> x1, Pallas kernels: none -> 2.09 us  [body(): pl.pallas_call(hand_on, out_shape=(jax.ShapeDtypeStruct((S13, IMG, D), BF...]
where the time goes in v3:
time: 63.9 us; the launch traced here: 63.7 us
  Pallas kernels  63.1 us (99%)
  between operations  0.64 us (1%)
    pallas_call x1, Pallas kernels, body(): pl.pallas_call(kernel, out_shape=(jax.ShapeDtypeStruct((S13, IMG, D), BF1...  61 us
    pallas_call x1, Pallas kernels, body(): pl.pallas_call(hand_on, out_shape=(jax.ShapeDtypeStruct((S13, IMG, D), BF...  2.09 us

profile of v3, /device:TPU:1, one launch (start us, length us, event | category | flops | bytes accessed | tf_op | source)
XLA Modules:
  0.0 63.7 jit_solution(7490133604915156025)
XLA Ops:
  0.6 61.0 %shard_map.140 = (bf16[13,8,1920]{2,1,0:T(8,128)(2,1)}, bf16[8,16,1920]{2,1,0:T(8,128)(2,1)}) custom-call(s32[8]{0:T(128)} %labels_hbm.1, f32[4]{0:T(128)} %scale_hbm.1, s32[13,8,13]{2,1,0:T(8,128)} %bitcast.21, bf16[8,16,2,256]{3,2,1,0:T(2,128)(2,1)} %cache_hbm.1, f32[8,1,512]{2,1,0:T(1,128)} %features_hbm.1, f32[1920]{0:T(1024)} %bias_hbm.1, ...), custom_call_target="tpu_custom_call" | custom-call | flops 3000000000 | bytes 12000000 | tf_op jit(solution)/shard_map/pallas_call | solution.py:670
  61.6 2.1 %shard_map.141 = (bf16[13,8,1920]{2,1,0:T(8,128)(2,1)}, bf16[8,16,1920]{2,1,0:T(8,128)(2,1)}) custom-call(bf16[13,8,1920]{2,1,0:T(8,128)(2,1)} %get-tuple-element.6.a_ref, bf16[8,16,1920]{2,1,0:T(8,128)(2,1)} %get-tuple-element.7.b_ref), custom_call_target="tpu_custom_call" | custom-call | bytes 1800000 | tf_op jit(solution)/shard_map/pallas_call | solution.py:739

commit v4 on v3

--- a/solution.py
+++ b/solution.py
@@ -22,6 +22,7 @@
 PADDED = SMALL + IMG
 ROWS = 2 * LARGE + PADDED
 SPAN = 512
+PART = 512
 VIA_X = 768
 WIDE = 1024
 SECOND = D - WIDE
@@ -71,9 +72,9 @@
     thirteen, table, codebook, embed, qkv, wout,
     cache_send, cache_recv, mod_a, mod_b, mod, far_position, far_features, id_lanes, xhat, xmod,
     small_send, small_near, small_far, large_send, large_near,
-    weights, vext, att_small, att_large, small_recv, large_recv, small_all, large_all,
+    weights, vext, att_small, att_large, small_recv, large_recv, small_all, large_all, both_all,
     local_sem,
-    ma_s, ma_r, mb_s, mb_r, fp_s, fp_r, ca_s, ca_r, sn_s, sn_r, sf_s, sf_r, ln_s, ln_r,
+    ma_s, ma_r, mb_s, mb_r, fp_s, fp_r, sp_s, sp_r, ca_s, ca_r, sn_s, sn_r, sf_s, sf_r, ln_s, ln_r,
     as_s, as_r, al_s, al_r, fs_s, fl_s,
     wz_s, wz_r, ay_s, ay_r, bx_s, bx_r, ax_s, ax_r, by_s, by_r, wc_s, wc_r,
 ):
@@ -148,6 +149,10 @@
         to = (u + d) % HALF
         return remote(mod_b.at[u], mod_b.at[u], mb_s.at[to], mb_r.at[u], seq=in_half(to))
 
+    def spread_copy(d):
+        to = (x + d) % DPS
+        return remote(far_position.at[x], far_position.at[x], sp_s.at[to], sp_r.at[x], dp=to)
+
     def cache_copy(d):
         to = (seq + d) % 16
         return remote(cache_send.at[to % HALF], cache_recv.at[seq], ca_s.at[to], ca_r.at[seq], seq=to)
@@ -283,6 +288,7 @@
     groups = {
         "mod_a": (1, HEADSETS, mod_a_copy, lambda d: (mod_a.at[(h + d) % HEADSETS], ma_r.at[(h + d) % HEADSETS])),
         "mod_b": (1, HALF, mod_b_copy, lambda d: (mod_b.at[(u + d) % HALF], mb_r.at[(u + d) % HALF])),
+        "spread": (1, DPS, spread_copy, lambda d: (far_position.at[(x + d) % DPS], sp_r.at[(x + d) % DPS])),
         "cache": (1, 16, cache_copy, lambda d: (cache_recv.at[(seq + d) % 16], ca_r.at[(seq + d) % 16])),
         "small_near": (
             1, HALF, small_near_copy, lambda d: (small_near.at[(u + d) % HALF], sn_r.at[(u + d) % HALF]),
@@ -360,7 +366,10 @@
         over(low, high, lambda d: copy(d).wait_send())
 
     partner = [
-        remote(position.at[0], far_position, fp_s.at[0], fp_r.at[0], seq=in_other(u)),
+        remote(
+            position.at[0, :, pl.ds(pl.multiple_of(x * PART - (x // 3) * 128, 128), PART)], far_position.at[x],
+            fp_s.at[0], fp_r.at[0], seq=in_other(u),
+        ),
         remote(feature_sum, far_features, fp_s.at[1], fp_r.at[1], seq=in_other(u)),
     ]
 
@@ -394,12 +403,12 @@
 
     pl.semaphore_wait(barrier, HEADSETS * HALF - 1 + HALF + DPS - 1)
     start("mod_a")
-    for copy in partner:
-        copy.start()
     loads["out0"].wait()
     loads["out1"].wait()
     start("wz")
     start("vz")
+    for copy in partner:
+        copy.start()
 
     taps = []
     for n, row in enumerate((seq, (seq + HALF) % 16)):
@@ -472,10 +481,14 @@
             row = xhat[at : at + 16, :] + bias_row + pair
             xhat[at : at + 16, :] = layer_norm(row.astype(BF16).astype(F32))
 
+    partner[0].wait_recv()
+    start("spread")
     embedded(0, feature_sum[:, 0, :], looked[0:SMALL], position[0])
-    for copy in partner:
-        copy.wait_recv()
-    embedded(LARGE, far_features[:, 0, :], looked[SMALL : 2 * SMALL], far_position[...])
+    arrive("spread")
+    partner[1].wait_recv()
+    far_rows = [far_position[k] for k in range(DPS)]
+    far_rows[DPS - 1] = far_rows[DPS - 1][:, DPS * PART - D :]
+    embedded(LARGE, far_features[:, 0, :], looked[SMALL : 2 * SMALL], jnp.concatenate(far_rows, axis=1))
 
     arrive("wz")
     arrive("vz")
@@ -634,8 +647,23 @@
         large_all[:, k * W : (k + 1) * W] = large_recv[k].reshape(LARGE, W)
     project_large(core)
     arrive("wc")
-    project_small(1 - core)
-    project_large(1 - core)
+    both_all[0:PADDED, :] = small_all[...]
+    both_all[PADDED:, :] = large_all[...]
+
+    def project_both(i):
+        side = 1 - core
+        inner = pl.multiple_of(i * W, W)
+        outer = pl.ds(pl.multiple_of(side * SECOND + inner, 128), W)
+        branch = dot(both_all[...], wout[side, :, pl.ds(inner, W)])
+        gate = mod[2, :, outer]
+        for j in range(S13):
+            rows = gate * branch[j * IMG : (j + 1) * IMG]
+            o13[j, :, outer] = jnp.where(kept, rows, jnp.zeros_like(rows)).astype(BF16)
+        for b in range(IMG):
+            rows = branch[PADDED + b * S16 : PADDED + (b + 1) * S16]
+            o16[b, :, outer] = (gate[b : b + 1] * rows).astype(BF16)
+
+    over(0, WIDE // W, project_both)
 
     for copy in partner:
         copy.wait_send()
@@ -694,7 +722,7 @@
             pltpu.VMEM((HEADSETS, 32, W), BF16),
             pltpu.VMEM((HALF, 32, W), BF16),
             pltpu.VMEM((3, IMG, D), F32),
-            pltpu.VMEM((S16, D), BF16),
+            pltpu.VMEM((DPS, S16, PART), BF16),
             pltpu.VMEM((IMG, 1, S16 * 32), F32),
             pltpu.VMEM((4, S13, IMG, 128), jnp.int32),
             pltpu.VMEM((ROWS, D), F32),
@@ -712,10 +740,11 @@
             pltpu.VMEM((HEADSETS, HALF, TOK, W), BF16),
             pltpu.VMEM((PADDED, HEADSETS * W), BF16),
             pltpu.VMEM((LARGE, HEADSETS * W), BF16),
+            pltpu.VMEM((PADDED + LARGE, HEADSETS * W), BF16),
             dma((14,)),
         ]
         + [dma((n,)) for n in (
-            4, 4, 8, 8, 2, 2, 16, 16, 8, 8, 8, 8, 8, 8, 32, 32, 32, 32, 8, 8, 8, 8, 16, 16, 16, 16, 16, 16, 16, 16, 4, 4
+            4, 4, 8, 8, 2, 2, 4, 4, 16, 16, 8, 8, 8, 8, 8, 8, 32, 32, 32, 32, 8, 8, 8, 8, 16, 16, 16, 16, 16, 16, 16, 16, 4, 4
         )],
         compiler_params=pltpu.CompilerParams(
             collective_id=0, has_side_effects=True, vmem_limit_bytes=VMEM_LIMIT

time: 63.9 us -> 60.2 us (0.942)
  Pallas kernels: 63.1 us -> 59.1 us
    pallas_call x1, Pallas kernels: 61 us -> 57 us  [body(): pl.pallas_call(kernel, out_shape=(jax.ShapeDtypeStruct((S13, IMG, D), BF1...]
where the time goes in v4:
time: 60.2 us; the launch traced here: 59.7 us
  Pallas kernels  59.1 us (98%)
  between operations  0.64 us (1%)
    pallas_call x1, Pallas kernels, body(): pl.pallas_call(kernel, out_shape=(jax.ShapeDtypeStruct((S13, IMG, D), BF1...  57 us
    pallas_call x1, Pallas kernels, body(): pl.pallas_call(hand_on, out_shape=(jax.ShapeDtypeStruct((S13, IMG, D), BF...  2.09 us

profile of v4, /device:TPU:1, one launch (start us, length us, event | category | flops | bytes accessed | tf_op | source)
XLA Modules:
  0.0 59.7 jit_solution(3538197710722583973)
XLA Ops:
  0.6 57.0 %shard_map.140 = (bf16[13,8,1920]{2,1,0:T(8,128)(2,1)}, bf16[8,16,1920]{2,1,0:T(8,128)(2,1)}) custom-call(s32[8]{0:T(128)} %labels_hbm.1, f32[4]{0:T(128)} %scale_hbm.1, s32[13,8,13]{2,1,0:T(8,128)} %bitcast.21, bf16[8,16,2,256]{3,2,1,0:T(2,128)(2,1)} %cache_hbm.1, f32[8,1,512]{2,1,0:T(1,128)} %features_hbm.1, f32[1920]{0:T(1024)} %bias_hbm.1, ...), custom_call_target="tpu_custom_call" | custom-call | flops 3000000000 | bytes 12000000 | tf_op jit(solution)/shard_map/pallas_call | solution.py:698
  57.6 2.1 %shard_map.141 = (bf16[13,8,1920]{2,1,0:T(8,128)(2,1)}, bf16[8,16,1920]{2,1,0:T(8,128)(2,1)}) custom-call(bf16[13,8,1920]{2,1,0:T(8,128)(2,1)} %get-tuple-element.6.a_ref, bf16[8,16,1920]{2,1,0:T(8,128)(2,1)} %get-tuple-element.7.b_ref), custom_call_target="tpu_custom_call" | custom-call | bytes 1800000 | tf_op jit(solution)/shard_map/pallas_call | solution.py:768

commit v5 on v4

--- a/solution.py
+++ b/solution.py
@@ -67,8 +67,8 @@
 def kernel(
     labels_hbm, scale_hbm, ids_hbm, cache_hbm, features_hbm, bias_hbm, position_hbm,
     thirteen_hbm, table_hbm, codebook_hbm, embed_hbm, qkv_hbm, out_hbm,
-    o13, o16,
-    labels, head_scale, ids, cache, feature_sum, bias, position,
+    o13_hbm, o16_hbm,
+    o13, o16, labels, head_scale, ids, cache, feature_sum, bias, position,
     thirteen, table, codebook, embed, qkv, wout,
     cache_send, cache_recv, mod_a, mod_b, mod, far_position, far_features, id_lanes, xhat, xmod,
     small_send, small_near, small_far, large_send, large_near,
@@ -638,6 +638,13 @@
 
         over(0, WIDE // W, step)
 
+    def written(first, width, sem):
+        where = pl.ds(pl.multiple_of(first, 128), width)
+        return [
+            pltpu.make_async_copy(o13.at[:, :, where], o13_hbm.at[:, :, where], local_sem.at[sem]),
+            pltpu.make_async_copy(o16.at[:, :, where], o16_hbm.at[:, :, where], local_sem.at[sem + 1]),
+        ]
+
     gathers[0].arrive()
     for k in range(HEADSETS):
         small_all[:, k * W : (k + 1) * W] = dot(to_row, small_recv[k].reshape(LARGE, W)).astype(BF16)
@@ -646,15 +653,18 @@
     for k in range(HEADSETS):
         large_all[:, k * W : (k + 1) * W] = large_recv[k].reshape(LARGE, W)
     project_large(core)
+    write_own = written(core * SECOND, WIDE, 14)
+    for copy in write_own:
+        copy.start()
     arrive("wc")
     both_all[0:PADDED, :] = small_all[...]
     both_all[PADDED:, :] = large_all[...]
 
-    def project_both(i):
+    def project_both(first, width):
         side = 1 - core
-        inner = pl.multiple_of(i * W, W)
-        outer = pl.ds(pl.multiple_of(side * SECOND + inner, 128), W)
-        branch = dot(both_all[...], wout[side, :, pl.ds(inner, W)])
+        inner = pl.multiple_of((1 - core) * (WIDE - SECOND) + first, 128)
+        outer = pl.ds(pl.multiple_of(side * SECOND + inner, 128), width)
+        branch = dot(both_all[...], wout[side, :, pl.ds(inner, width)])
         gate = mod[2, :, outer]
         for j in range(S13):
             rows = gate * branch[j * IMG : (j + 1) * IMG]
@@ -663,7 +673,11 @@
             rows = branch[PADDED + b * S16 : PADDED + (b + 1) * S16]
             o16[b, :, outer] = (gate[b : b + 1] * rows).astype(BF16)
 
-    over(0, WIDE // W, project_both)
+    over(0, SECOND // W, lambda i: project_both(i * W, W))
+    project_both(SECOND // W * W, SECOND % W)
+    write_other = written((1 - core) * WIDE, SECOND, 16)
+    for copy in write_other:
+        copy.start()
 
     for copy in partner:
         copy.wait_send()
@@ -671,6 +685,8 @@
         sent(name)
     for gather in gathers:
         gather.sent()
+    for copy in write_own + write_other:
+        copy.wait()
 
 
 def hand_on(a_ref, b_ref, a_out, b_out, sem):
@@ -702,8 +718,10 @@
             jax.ShapeDtypeStruct((IMG, S16, D), BF16),
         ),
         in_specs=[anywhere] * 13,
-        out_specs=(vmem, vmem),
+        out_specs=(anywhere, anywhere),
         scratch_shapes=[
+            pltpu.VMEM((S13, IMG, D), BF16),
+            pltpu.VMEM((IMG, S16, D), BF16),
             pltpu.SMEM((IMG,), jnp.int32),
             pltpu.SMEM(head_scale.shape, F32),
             pltpu.VMEM((S13, IMG, S13), jnp.int32),
@@ -741,7 +759,7 @@
             pltpu.VMEM((PADDED, HEADSETS * W), BF16),
             pltpu.VMEM((LARGE, HEADSETS * W), BF16),
             pltpu.VMEM((PADDED + LARGE, HEADSETS * W), BF16),
-            dma((14,)),
+            dma((18,)),
         ]
         + [dma((n,)) for n in (
             4, 4, 8, 8, 2, 2, 4, 4, 16, 16, 8, 8, 8, 8, 8, 8, 32, 32, 32, 32, 8, 8, 8, 8, 16, 16, 16, 16, 16, 16, 16, 16, 4, 4

time: 60.2 us -> 59.3 us (0.985)
  Pallas kernels: 59.1 us -> 58.2 us
    pallas_call x1, Pallas kernels: 57 us -> 56.1 us  [body(): pl.pallas_call(kernel, out_shape=(jax.ShapeDtypeStruct((S13, IMG, D), BF1...]
where the time goes in v5:
time: 59.3 us; the launch traced here: 58.8 us
  Pallas kernels  58.2 us (98%)
  between operations  0.64 us (1%)
    pallas_call x1, Pallas kernels, body(): pl.pallas_call(kernel, out_shape=(jax.ShapeDtypeStruct((S13, IMG, D), BF1...  56.1 us
    pallas_call x1, Pallas kernels, body(): pl.pallas_call(hand_on, out_shape=(jax.ShapeDtypeStruct((S13, IMG, D), BF...  2.09 us

profile of v5, /device:TPU:1, one launch (start us, length us, event | category | flops | bytes accessed | tf_op | source)
XLA Modules:
  0.0 58.8 jit_solution(1413983340535602682)
XLA Ops:
  0.6 56.1 %shard_map.140 = (bf16[13,8,1920]{2,1,0:T(8,128)(2,1)}, bf16[8,16,1920]{2,1,0:T(8,128)(2,1)}) custom-call(s32[8]{0:T(128)} %labels_hbm.1, f32[4]{0:T(128)} %scale_hbm.1, s32[13,8,13]{2,1,0:T(8,128)} %bitcast.21, bf16[8,16,2,256]{3,2,1,0:T(2,128)(2,1)} %cache_hbm.1, f32[8,1,512]{2,1,0:T(1,128)} %features_hbm.1, f32[1920]{0:T(1024)} %bias_hbm.1, ...), custom_call_target="tpu_custom_call" | custom-call | flops 3000000000 | bytes 12000000 | tf_op jit(solution)/shard_map/pallas_call | solution.py:714
  56.7 2.1 %shard_map.141 = (bf16[13,8,1920]{2,1,0:T(8,128)(2,1)}, bf16[8,16,1920]{2,1,0:T(8,128)(2,1)}) custom-call(bf16[13,8,1920]{2,1,0:T(8,128)(2,1)} %get-tuple-element.6.a_ref, bf16[8,16,1920]{2,1,0:T(8,128)(2,1)} %get-tuple-element.7.b_ref), custom_call_target="tpu_custom_call" | custom-call | bytes 1800000 | tf_op jit(solution)/shard_map/pallas_call | solution.py:786
